TPU v7x, 256 devices: a whole 4x4x8 slice. The times are simulated.
256 devices in a mesh: row: 16 (over x_hi, z), col: 16 (over x_lo, y, core).
Axes of the slice: x: 4 (x_hi: 2, x_lo: 2; x = x_hi * 2 + x_lo), y: 4, z: 8, core: 2. Of those that a mesh axis runs over, the one named last changes fastest.
Arguments:
- pair: float32 [768, 768, 128], P('row', 'col'), may hold values from -6 to 6
- pair_mask: int32 [768, 768], P('row', 'col'), may hold values from 0 to 1, as said below
- ln_gain: float32 [128], replicated, may hold values from 0.25 to 1.75
- ln_bias: float32 [128], replicated, may hold values from -3 to 3
- w_proj: bfloat16 [128, 512], replicated, may hold values from -0.5 to 0.5
- w_gate: bfloat16 [128, 128], replicated, may hold values from -0.5 to 0.5
- out_gain: float32 [128], replicated, may hold values from 0.25 to 1.75
- out_bias: float32 [128], replicated, may hold values from -3 to 3
- w_out: bfloat16 [128, 128], replicated, may hold values from -0.5 to 0.5
Outputs:
- update: float32 [768, 768, 128], P('row', 'col')
Inputs may be any that keep to these rules, and one draw needn't show every extreme that they name: pair_mask[i, j] = real[i] * real[j] for a 0/1 flag real of each of the 768 tokens; token 0 is real and token 767 is padding.
All inputs are finite; a program needn't handle non-finite values.
Results may differ from a plain program's by a relative error of at most 0.0033.
Values may be sent and summed in bfloat16 or wider, within the bound.
No kernel may reach another device: no remote copies, remote signals or barrier semaphores. Data moves between devices by JAX's collectives and lax.ppermute only.
A program may use at most 128 MiB of HBM per device.

v0:
```python
import jax
import jax.numpy as jnp
from jax import lax
from jax.sharding import PartitionSpec as P


def layer_norm(values, gain, bias):
    mean = jnp.mean(values, axis=-1, keepdims=True)
    centred = values - mean
    var = jnp.mean(centred * centred, axis=-1, keepdims=True)
    return centred * lax.rsqrt(var + 1e-05) * gain + bias


def per_device(pair, pair_mask, ln_gain, ln_bias, w_proj, w_gate, out_gain, out_bias, w_out):
    rows, cols, chan = pair.shape
    hidden = w_out.shape[0]
    normed = layer_norm(pair, ln_gain, ln_bias).astype(jnp.bfloat16)
    flat = normed.reshape(rows * cols, chan)
    proj = jnp.dot(flat, w_proj, preferred_element_type=jnp.float32).reshape(rows, cols, 4, hidden)
    keep = pair_mask.astype(jnp.float32)[:, :, None]
    left = (keep * jax.nn.sigmoid(proj[:, :, 0]) * proj[:, :, 1]).astype(jnp.bfloat16)
    right = (keep * jax.nn.sigmoid(proj[:, :, 2]) * proj[:, :, 3]).astype(jnp.bfloat16)
    right_all = lax.all_gather(right, "row", axis=0, tiled=True)
    right_mine = lax.all_to_all(right_all, "col", split_axis=0, concat_axis=1, tiled=True)
    mixed = jnp.einsum(
        "ikh,jkh->ijh",
        lax.all_gather(left, "col", axis=1, tiled=True),
        right_mine,
        preferred_element_type=jnp.float32,
    )
    mixed_norm = layer_norm(mixed, out_gain, out_bias).astype(jnp.bfloat16)
    projected = jnp.dot(
        mixed_norm.reshape(rows * cols, hidden), w_out, preferred_element_type=jnp.float32
    )
    gating = jax.nn.sigmoid(jnp.dot(flat, w_gate, preferred_element_type=jnp.float32))
    return (gating * projected).reshape(rows, cols, chan)


def solution(mesh):
    return jax.shard_map(
        per_device,
        mesh=mesh,
        in_specs=(P("row", "col", None), P("row", "col"), P(), P(), P(), P(), P(), P(), P()),
        out_specs=P("row", "col", None),
        check_vma=False,
    )
```

profile of v0, /device:TPU:19, one launch (start us, length us, event | category | flops | bytes accessed | tf_op | source)
XLA Modules:
  0.0 389.3 jit_solution(4326955354253959201)
XLA Ops:
  6.5 0.0 copy-start
  6.5 0.0 copy-start.2
  6.5 0.0 copy-start.4
  6.5 0.0 copy-start.6
  6.5 0.0 copy-start.8
  6.5 0.0 copy-start.7
  6.6 0.0 all-gather.3.cloned.1.call-start
  6.6 1.7 reduce_sum.36
  8.4 0.0 copy-done.2
  8.4 0.7 multiply_reduce_fusion.1
  9.1 0.0 copy-done.4
  9.1 0.1 copy.60
  9.2 0.0 copy-done.6
  9.2 0.0 copy-done.8
  9.3 0.0 copy-done.7
  9.3 0.8 add_convert_fusion.1
  10.1 0.8 fusion.19
  10.8 1.6 fusion.4
  12.4 0.0 all-gather.3.cloned.1.call-update
  12.4 0.0 all-gather.5.cloned.1.call-start
  12.5 0.7 all-gather.5.cloned.1.call-update
  13.2 147.2 %all-gather.3.cloned.1.call-done = bf16[768,48,128]{2,1,0:T(8,128)(2,1)} async-done(((bf16[48,48,128]{2,1,0:T(8,128)(2,1)}), bf16[768,48,128]{2,1,0:T(8,128)(2,1)}) %all-gather.3.cloned.1.call-update) | async-done | bytes 9437200 | tf_op jit(solution)/shard_map/all_gather | solution.py:23
  160.4 6.7 %all-to-all-start = ((bf16[768,48,128]{2,1,0:T(8,128)(2,1)}), bf16[768,48,128]{2,1,0:T(8,128)(2,1)}, u32[]{:S(2)}, u32[]{:S(2)}) async-start(bf16[768,48,128]{2,1,0:T(8,128)(2,1)} %all-gather.3.cloned.1.call-done), calls=%async_computation | async-start | bytes 18874368 | tf_op jit(solution)/shard_map/all_to_all | solution.py:24
  167.1 0.0 copy-done
  167.1 1.5 fusion.2
  168.6 162.6 %all-gather.5.cloned.1.call-done = bf16[48,768,128]{2,1,0:T(8,128)(2,1)} async-done(((bf16[48,48,128]{2,1,0:T(8,128)(2,1)}), bf16[48,768,128]{2,1,0:T(8,128)(2,1)}) %all-gather.5.cloned.1.call-update) | async-done | bytes 9437200 | tf_op jit(solution)/shard_map/all_gather | solution.py:27
  331.2 12.9 %copy.53 = bf16[48,768,128]{1,0,2:T(8,128)(2,1)} copy(bf16[48,768,128]{2,1,0:T(8,128)(2,1)} %all-gather.5.cloned.1.call-done) | data formatting | bytes 18874368 | tf_op jit(solution)/shard_map/all_gather | solution.py:27
  344.1 0.0 all-to-all-done
  344.1 10.1 %copy.50 = bf16[48,16,48,128]{3,2,1,0:T(8,128)(2,1)} copy(bf16[48,16,48,128]{3,2,0,1:T(8,128)(2,1)} %bitcast.9) | data formatting | bytes 18874368 | tf_op jit(solution)/shard_map/all_to_all | solution.py:24
  354.2 12.9 %copy.52 = bf16[48,768,128]{1,0,2:T(8,128)(2,1)} copy(bf16[48,768,128]{2,1,0:T(8,128)(2,1)} %bitcast.88) | data formatting | bytes 18874368 | tf_op jit(solution)/shard_map/all_to_all | solution.py:24
  367.2 9.0 %bitcast_reduce_fusion = (f32[48,48]{0,1:T(8,128)S(1)}, f32[128,48,48]{2,1,0:T(8,128)S(1)}) fusion(bf16[48,768,128]{1,0,2:T(8,128)(2,1)} %copy.52, bf16[48,768,128]{1,0,2:T(8,128)(2,1)} %copy.53), kind=kOutput, calls=%fused_computation.6 | convolution fusion | flops 453277440 | bytes 20063232 | tf_op jit(solution)/shard_map/ikh,jkh->ijh/dot_general | solution.py:25
  376.1 0.1 copy.54
  376.2 0.1 copy.55
  376.3 0.0 copy-start.9
  376.3 0.0 copy-start.10
  376.3 0.5 multiply_reduce_fusion
  376.8 0.1 copy.56
  376.9 0.1 copy.57
  377.0 0.0 copy-done.9
  377.0 0.0 copy-done.10
  377.0 1.7 add_convert_fusion
  378.7 0.0 copy-start.3
  378.7 0.0 copy-start.5
  378.7 2.4 copy.58
  381.1 0.0 copy-start.1
  381.1 0.0 copy-done.3
  381.1 0.0 copy-done.5
  381.1 1.3 convolution_multiply_fusion
  382.4 0.0 copy-done.1
  (5 shorter events, 0.0 us)
Async XLA Ops:
  6.5 160.6 %copy-start = (bf16[128,128]{1,0:T(8,128)(2,1)S(1)}, bf16[128,128]{1,0:T(8,128)(2,1)}, u32[]{:S(2)}) copy-start(bf16[128,128]{1,0:T(8,128)(2,1)} %param.14) | copy-start | bytes 98308
  6.5 1.8 copy-start.2
  6.5 2.6 copy-start.4
  6.5 2.7 copy-start.6
  6.5 2.7 copy-start.8
  6.5 2.7 copy-start.7
  6.6 153.8 %all-gather.3.cloned.1.call-start = ((), (), s32[]{:S(2)}) async-start(), calls=%async_computation.1 | async-start | bytes 10027008 | tf_op jit(solution)/shard_map/all_gather | solution.py:23
  12.4 318.7 %all-gather.5.cloned.1.call-start = ((), (), s32[]{:S(2)}) async-start(), calls=%async_computation.2 | async-start | bytes 10027008 | tf_op jit(solution)/shard_map/all_gather | solution.py:27
  160.4 183.8 %all-to-all-start = ((bf16[768,48,128]{2,1,0:T(8,128)(2,1)}), bf16[768,48,128]{2,1,0:T(8,128)(2,1)}, u32[]{:S(2)}, u32[]{:S(2)}) async-start(bf16[768,48,128]{2,1,0:T(8,128)(2,1)} %all-gather.3.cloned.1.call-done), calls=%async_computation | async-start | bytes 18874368 | tf_op jit(solution)/shard_map/all_to_all | solution.py:24
  376.3 0.7 copy-start.9
  376.3 0.7 copy-start.10
  378.7 2.4 copy-start.3
  378.7 2.4 copy-start.5
  381.1 1.3 copy-start.1
Sparse Core Ops, SparseCore 0:
  12.6 147.7 all-gather.2
  162.2 168.9 all-gather.4
where the time goes:
time: 390 us; the launch traced here: 389 us
  waiting for transfers between devices  310 us (79%)
  local copies, waits for them, and re-layouts  38.8 us (10%)
  between operations  13.6 us (3%)
  matrix products  12.5 us (3%)
  other arithmetic  7.01 us (2%)
  starting transfers between devices  6.81 us (2%)
    all_gather x1, waiting for transfers between devices, per_device(): lax.all_gather(left, 'col', axis=1, tiled=True)  163 us
    all_gather x1, waiting for transfers between devices, per_device(): right_all = lax.all_gather(right, 'row', axis=0, tiled=True)  147 us
    all_to_all x2, local copies, waits for them, and re-layouts, per_device(): lax.all_to_all(right_all, 'col', split_axis=0, concat_axis=1, tiled=True)  23.1 us
    all_gather x1, local copies, waits for them, and re-layouts, per_device(): lax.all_gather(left, 'col', axis=1, tiled=True)  12.9 us
    dot_general x1, matrix products, per_device(): jnp.einsum('ikh,jkh->ijh', lax.all_gather(left, 'col', axis=1, tiled=True...  8.96 us
  transfers between devices with their start and end apart: 3, of which 2 were waited for; matrix products, arithmetic and copies ran while one was open for 4% of the time, Pallas kernels for 0%

commit v1 on v0

v1 whole, which is shorter than its diff:
```python
import jax
import jax.numpy as jnp
from jax import lax
from jax.experimental import pallas as pl
from jax.experimental.pallas import tpu as pltpu
from jax.sharding import Mesh, PartitionSpec as P

EPS = 1e-05
ROW = ("xh", "zh", "zl")
COL = ("xl", "y", "core")
OUT = ("zl", "xl", "y", "xh", "zh")
BACK = ("zl", "xh", "zh", "xl", "y")
F32, BF16 = jnp.float32, jnp.bfloat16


def sigmoid(x):
    return 0.5 * jnp.tanh(0.5 * x) + 0.5


def layer_norm(x, gain, bias, axis):
    mean = jnp.mean(x, axis=axis, keepdims=True)
    centred = x - mean
    var = jnp.mean(centred * centred, axis=axis, keepdims=True)
    return centred * lax.rsqrt(var + EPS) * gain + bias


def project_kernel(pair_ref, mask_ref, gain_ref, bias_ref, w_ref, out_ref, wt_ref):
    @pl.when(pl.program_id(0) == 0)
    def _():
        wt_ref[...] = w_ref[...].astype(F32).T.astype(BF16)

    x = pair_ref[...].reshape(8 * 48, 128)
    normed = layer_norm(x, gain_ref[...], bias_ref[...], -1).astype(BF16)
    normed = normed.reshape(8, 3, 16, 128).transpose(1, 0, 2, 3).reshape(384, 128)
    lane = lax.broadcasted_iota(jnp.int32, (48, 384), 1)
    row = lax.broadcasted_iota(jnp.int32, (48, 384), 0)
    spread = (lane // 128 * 16 + lane % 16 == row).astype(F32)
    keep = jnp.dot(mask_ref[...].astype(F32), spread, preferred_element_type=F32)
    lane8 = lax.broadcasted_iota(jnp.int32, (8, 384), 1)
    row8 = lax.broadcasted_iota(jnp.int32, (8, 384), 0)
    keep = jnp.sum(jnp.where(lane8 // 16 % 8 == row8, keep, 0.0), axis=0, keepdims=True)
    nt = (((1,), (1,)), ((), ()))
    for side in range(2):
        gate = lax.dot_general(wt_ref[side * 256 : side * 256 + 128, :], normed, nt, preferred_element_type=F32)
        value = lax.dot_general(wt_ref[side * 256 + 128 : side * 256 + 256, :], normed, nt, preferred_element_type=F32)
        out_ref[side, 0] = (keep * sigmoid(gate) * value).astype(BF16)


def project(pair, mask, gain, bias, w_proj):
    full = lambda *shape: pl.BlockSpec(shape, lambda i: (0,) * len(shape))
    return pl.pallas_call(
        project_kernel,
        grid=(6,),
        out_shape=jax.ShapeDtypeStruct((2, 2, 128, 1152), BF16),
        in_specs=[
            pl.BlockSpec((8, 48, 128), lambda i: (i, 0, 0)),
            pl.BlockSpec((8, 48), lambda i: (i, 0)),
            full(1, 128),
            full(1, 128),
            full(128, 512),
        ],
        out_specs=pl.BlockSpec((2, 1, 128, 384), lambda i: (0, i // 3, 0, i % 3)),
        scratch_shapes=[pltpu.VMEM((512, 128), BF16)],
        name="project",
    )(pair, mask, gain, bias, w_proj)


def swap_blocks(arrays, block):
    arrays = list(arrays)
    lane = lax.broadcasted_iota(jnp.int32, arrays[0].shape, arrays[0].ndim - 1)
    d = len(arrays) // 2
    while d:
        shift = d * block
        low = (lane & shift) == 0
        for a in range(len(arrays)):
            if a & d == 0:
                p, q = arrays[a], arrays[a + d]
                arrays[a] = jnp.where(low, p, pltpu.roll(q, shift, p.ndim - 1))
                arrays[a + d] = jnp.where(low, pltpu.roll(p, 128 - shift, p.ndim - 1), q)
        d //= 2
    return arrays


def gather_kernel(core_ref, recv_ref, send_ref, keep_ref):
    core = core_ref[0]
    for side in range(2):
        for s in range(18):
            ii_hi, kk_hi = s // 3, s % 3
            tile = recv_ref[side * 2 + s // 9, :, s % 9 * 128 : s % 9 * 128 + 128].astype(F32).reshape(2, 8, 8, 128)
            lanes = slice(kk_hi * 128, kk_hi * 128 + 128)
            for zl in range(2):
                rows = jnp.stack(swap_blocks([tile[zl, c] for c in range(8)], 16))
                tile_rows = rows
                if side == 0:
                    out = tile_rows
                    if zl == 0:
                        first = out
                    else:
                        both = jnp.stack([first, out], axis=1).reshape(128, 128).astype(BF16)
                        send_ref[ii_hi * 128 : ii_hi * 128 + 128, lanes] = both
                else:
                    out = tile_rows.reshape(64, 128).astype(BF16)

                    @pl.when(core == zl)
                    def _():
                        keep_ref[ii_hi * 64 : ii_hi * 64 + 64, lanes] = out

                    @pl.when(core != zl)
                    def _():
                        send_ref[768 + ii_hi * 64 : 768 + ii_hi * 64 + 64, lanes] = out


def gather(core, recv):
    return pl.pallas_call(
        gather_kernel,
        out_shape=(jax.ShapeDtypeStruct((1152, 384), BF16), jax.ShapeDtypeStruct((384, 384), BF16)),
        in_specs=[pl.BlockSpec(memory_space=pltpu.SMEM), pl.BlockSpec(memory_space=pltpu.VMEM)],
        out_specs=(pl.BlockSpec(memory_space=pltpu.VMEM), pl.BlockSpec(memory_space=pltpu.VMEM)),
        name="gather",
    )(core, recv)


def contract_kernel(mine_ref, other_ref, keep_ref, out_ref):
    nt = (((1,), (1,)), ((), ()))
    for i in range(6):
        cols = slice(i * 128, i * 128 + 128)
        mixed = lax.dot_general(keep_ref[...], mine_ref[cols, :], nt, preferred_element_type=F32)
        mixed += lax.dot_general(other_ref[768:, :], other_ref[cols, :], nt, preferred_element_type=F32)
        mixed = mixed.reshape(3, 16, 8, 128)
        for j in range(3):
            s = i * 3 + j
            out = jnp.stack(swap_blocks([mixed[j, a] for a in range(16)], 1))
            out_ref[s // 9, :, s % 9 * 128 : s % 9 * 128 + 128] = out.reshape(128, 128).astype(BF16)


def contract(mine, other, keep):
    return pl.pallas_call(
        contract_kernel,
        out_shape=jax.ShapeDtypeStruct((2, 128, 1152), BF16),
        name="contract",
    )(mine, other, keep)


def gate_kernel(pair_ref, gain_ref, bias_ref, w_ref, out_ref):
    x = pair_ref[...].reshape(8 * 48, 128)
    normed = layer_norm(x, gain_ref[...], bias_ref[...], -1).astype(BF16)
    gate = sigmoid(jnp.dot(normed, w_ref[...], preferred_element_type=F32))
    out_ref[...] = gate.reshape(8, 48, 128)


def gating(pair, gain, bias, w_gate):
    full = lambda *shape: pl.BlockSpec(shape, lambda i: (0,) * len(shape))
    return pl.pallas_call(
        gate_kernel,
        grid=(6,),
        out_shape=jax.ShapeDtypeStruct((48, 48, 128), F32),
        in_specs=[pl.BlockSpec((8, 48, 128), lambda i: (i, 0, 0)), full(1, 128), full(1, 128), full(128, 128)],
        out_specs=pl.BlockSpec((8, 48, 128), lambda i: (i, 0, 0)),
        cost_estimate=pl.CostEstimate(flops=75_000_000, bytes_accessed=2_400_000, transcendentals=300_000),
        name="gate",
    )(pair, gain, bias, w_gate)


def finish_kernel(mixed_ref, gate_ref, gain_ref, bias_ref, w_ref, out_ref):
    mixed = mixed_ref[0].astype(F32)
    normed = layer_norm(mixed, gain_ref[...], bias_ref[...], 0).astype(BF16)
    tn = (((0,), (0,)), ((), ()))
    projected = lax.dot_general(normed, w_ref[...], tn, preferred_element_type=F32)
    projected = projected.reshape(3, 8, 16, 128).transpose(1, 0, 2, 3).reshape(8, 48, 128)
    out_ref[...] = gate_ref[...] * projected


def finish(mixed, gate, gain, bias, w_out):
    full = lambda *shape: pl.BlockSpec(shape, lambda i: (0,) * len(shape))
    return pl.pallas_call(
        finish_kernel,
        grid=(6,),
        out_shape=jax.ShapeDtypeStruct((48, 48, 128), F32),
        in_specs=[
            pl.BlockSpec((1, 128, 384), lambda i: (i // 3, 0, i % 3)),
            pl.BlockSpec((8, 48, 128), lambda i: (i, 0, 0)),
            full(128, 1),
            full(128, 1),
            full(128, 128),
        ],
        out_specs=pl.BlockSpec((8, 48, 128), lambda i: (i, 0, 0)),
        name="finish",
    )(mixed, gate, gain, bias, w_out)


def per_device(pair, pair_mask, ln_gain, ln_bias, w_proj, w_gate, out_gain, out_bias, w_out):
    gain, bias = ln_gain.reshape(1, 128), ln_bias.reshape(1, 128)
    sent = project(pair, pair_mask, gain, bias, w_proj).reshape(4, 128, 1152)
    recv = lax.all_to_all(sent, OUT, 1, 1, tiled=True)
    gate = gating(pair, gain, bias, w_gate)
    core = lax.axis_index("core").astype(jnp.int32).reshape(1)
    mine, keep = gather(core, recv)
    other = lax.ppermute(mine, "core", [(0, 1), (1, 0)])
    mixed = contract(mine, other, keep)
    mixed = lax.all_to_all(mixed, BACK, 1, 1, tiled=True)
    swap = lambda v: v.reshape(2, 8, 8, -1).transpose(0, 2, 1, 3).reshape(128, -1)
    return finish(mixed, gate, swap(out_gain), swap(out_bias), swap(w_out))


def solution(mesh):
    fine = Mesh(mesh.devices.reshape(2, 4, 2, 2, 4, 2), ROW + COL)
    return jax.shard_map(
        per_device,
        mesh=fine,
        in_specs=(P(ROW, COL, None), P(ROW, COL), P(), P(), P(), P(), P(), P(), P()),
        out_specs=P(ROW, COL, None),
        check_vma=False,
    )
```

time: 390 us -> 117 us (0.30)
  the two profiles are of different devices: /device:TPU:19 before, /device:TPU:32 now
where the time goes in v1:
time: 117 us
  waiting for transfers between devices  49.4 us (42%)
  Pallas kernels  34 us (29%)
  starting transfers between devices  22.1 us (19%)
  local copies, waits for them, and re-layouts  11 us (9%)
    all_to_all x1, waiting for transfers between devices, per_device(): recv = lax.all_to_all(sent, OUT, 1, 1, tiled=True)  33.1 us
    all_to_all x1, starting transfers between devices, per_device(): recv = lax.all_to_all(sent, OUT, 1, 1, tiled=True)  15.3 us
    all_to_all x1, waiting for transfers between devices, per_device(): mixed = lax.all_to_all(mixed, BACK, 1, 1, tiled=True)  13.7 us
    pallas_call x1, Pallas kernels, gather(): pl.pallas_call(gather_kernel, out_shape=(jax.ShapeDtypeStruct((1152, 384)...  13.6 us
    all_to_all x1, starting transfers between devices, per_device(): mixed = lax.all_to_all(mixed, BACK, 1, 1, tiled=True)  6.79 us
    pallas_call x1, Pallas kernels, project(): pl.pallas_call(project_kernel, grid=(6,), out_shape=jax.ShapeDtypeStruct(...  5.93 us
    pallas_call x1, Pallas kernels, finish(): pl.pallas_call(finish_kernel, grid=(6,), out_shape=jax.ShapeDtypeStruct((...  5.37 us
    pallas_call x1, Pallas kernels, gating(): pl.pallas_call(gate_kernel, grid=(6,), out_shape=jax.ShapeDtypeStruct((48...  5.31 us
  transfers between devices with their start and end apart: 3, of which 3 were waited for; matrix products, arithmetic and copies ran while one was open for 2% of the time, Pallas kernels for 5%

profile of v1, /device:TPU:32, one launch (start us, length us, event | category | flops | bytes accessed | tf_op | source)
XLA Modules:
  0.0 116.6 jit_solution(10506300909755328108)
XLA Ops:
  0.0 5.9 %project.1 = bf16[2,2,128,1152]{3,2,1,0:T(8,128)(2,1)} custom-call(f32[48,48,128]{2,1,0:T(8,128)} %pair_ref.3, s32[48,48]{1,0:T(8,128)} %mask_ref.1, f32[1,128]{1,0:T(1,128)} %bitcast.23, f32[1,128]{1,0:T(1,128)} %bitcast.25, bf16[128,512]{1,0:T(8,128)(2,1)} %w_ref.2), custom_call_target="tpu_custom_call" | custom-call | tf_op jit(solution)/shard_map/project/pallas_call | solution.py:51
  5.9 3.2 %copy.15 = bf16[4,128,1152]{2,0,1:T(4,128)(2,1)} copy(bf16[4,128,1152]{2,1,0:T(8,128)(2,1)} %bitcast.18) | data formatting | bytes 2359296 | tf_op jit(solution)/shard_map/reshape | solution.py:193
  9.1 15.3 %all-to-all-start = ((bf16[4,128,1152]{2,0,1:T(4,128)(2,1)}), bf16[4,128,1152]{2,0,1:T(4,128)(2,1)S(1)}, u32[]{:S(2)}, u32[]{:S(2)}) async-start(bf16[4,128,1152]{2,0,1:T(4,128)(2,1)} %copy.15), calls=%async_computation | async-start | bytes 2359296 | tf_op jit(solution)/shard_map/all_to_all | solution.py:194
  24.5 33.1 %all-to-all-done = bf16[4,128,1152]{2,0,1:T(4,128)(2,1)S(1)} async-done(((bf16[4,128,1152]{2,0,1:T(4,128)(2,1)}), bf16[4,128,1152]{2,0,1:T(4,128)(2,1)S(1)}, u32[]{:S(2)}, u32[]{:S(2)}) %all-to-all-start) | async-done | bytes 1179680 | tf_op jit(solution)/shard_map/all_to_all | solution.py:194
  57.6 1.1 copy.16.recv_ref
  58.7 13.6 %gather.1 = (bf16[1152,384]{1,0:T(8,128)(2,1)}, bf16[384,384]{1,0:T(8,128)(2,1)}) custom-call(s32[1]{0:T(128)} %bitcast.core_ref, bf16[4,128,1152]{2,1,0:T(8,128)(2,1)} %copy.16.recv_ref), custom_call_target="tpu_custom_call" | custom-call | tf_op jit(solution)/shard_map/gather/pallas_call | solution.py:114
  72.4 0.0 collective-permute-start
  72.4 2.6 %collective-permute-done.other_ref = bf16[1152,384]{1,0:T(8,128)(2,1)S(1)} collective-permute-done((bf16[1152,384]{1,0:T(8,128)(2,1)}, bf16[1152,384]{1,0:T(8,128)(2,1)S(1)}, u32[]{:S(2)}, u32[]{:S(2)}) %collective-permute-start) | collective-permute-done | bytes 884768 | tf_op jit(solution)/shard_map/ppermute | solution.py:198
  75.0 0.0 copy-start
  75.0 0.9 copy-done
  75.9 3.7 %contract.1 = bf16[2,128,1152]{2,1,0:T(8,128)(2,1)} custom-call(bf16[1152,384]{1,0:T(8,128)(2,1)} %get-tuple-element.7.mine_ref, bf16[1152,384]{1,0:T(8,128)(2,1)} %copy-done, bf16[384,384]{1,0:T(8,128)(2,1)} %get-tuple-element.8.keep_ref), custom_call_target="tpu_custom_call" | custom-call | tf_op jit(solution)/shard_map/contract/pallas_call | solution.py:137
  79.6 0.0 copy-start.2
  79.6 0.0 copy-start.3
  79.6 0.0 copy-start.1
  79.7 2.5 %copy.17 = bf16[2,128,1152]{2,0,1:T(2,128)(2,1)} copy(bf16[2,128,1152]{2,1,0:T(8,128)(2,1)} %contract.1) | data formatting | bytes 1179648 | tf_op jit(solution)/shard_map/contract/pallas_call | solution.py:137
  82.2 6.8 %all-to-all-start.1 = ((bf16[2,128,1152]{2,0,1:T(2,128)(2,1)}), bf16[2,128,1152]{2,0,1:T(2,128)(2,1)S(1)}, u32[]{:S(2)}, u32[]{:S(2)}) async-start(bf16[2,128,1152]{2,0,1:T(2,128)(2,1)} %copy.17), calls=%async_computation.1 | async-start | bytes 1179648 | tf_op jit(solution)/shard_map/all_to_all | solution.py:200
  89.0 0.0 copy-done.2
  89.0 0.1 reshape.34
  89.1 0.1 copy.18
  89.1 0.0 copy-done.3
  89.1 0.1 reshape.36
  89.2 0.1 copy.19
  89.3 0.0 copy-done.1
  89.3 0.6 copy.20
  89.9 0.7 reshape.41.bias_ref
  90.6 0.7 reshape.40.gain_ref
  91.3 5.3 %gate.1.gate_ref = f32[48,48,128]{2,1,0:T(8,128)} custom-call(f32[48,48,128]{2,1,0:T(8,128)} %pair_ref.3, f32[1,128]{1,0:T(1,128)} %bitcast.24, f32[1,128]{1,0:T(1,128)} %bitcast.26, bf16[128,128]{1,0:T(8,128)(2,1)} %w_ref.3), custom_call_target="tpu_custom_call" | custom-call | flops 75000000 | bytes 2400000 | tf_op jit(solution)/shard_map/gate/pallas_call | solution.py:153
  96.6 13.7 %all-to-all-done.1 = bf16[2,128,1152]{2,0,1:T(2,128)(2,1)S(1)} async-done(((bf16[2,128,1152]{2,0,1:T(2,128)(2,1)}), bf16[2,128,1152]{2,0,1:T(2,128)(2,1)S(1)}, u32[]{:S(2)}, u32[]{:S(2)}) %all-to-all-start.1) | async-done | bytes 589856 | tf_op jit(solution)/shard_map/all_to_all | solution.py:200
  110.3 0.9 copy.21.mixed_ref
  111.2 5.4 %finish.1 = f32[48,48,128]{2,1,0:T(8,128)} custom-call(bf16[2,128,1152]{2,1,0:T(8,128)(2,1)} %copy.21.mixed_ref, f32[48,48,128]{2,1,0:T(8,128)} %gate.1.gate_ref, f32[128,1]{1,0:T(8,128)} %reshape.40.gain_ref, f32[128,1]{1,0:T(8,128)} %reshape.41.bias_ref, bf16[128,128]{1,0:T(8,128)(2,1)} %bitcast.19), custom_call_target="tpu_custom_call" | custom-call | tf_op jit(solution)/shard_map/finish/pallas_call | solution.py:175
Async XLA Ops:
  9.1 48.4 %all-to-all-start = ((bf16[4,128,1152]{2,0,1:T(4,128)(2,1)}), bf16[4,128,1152]{2,0,1:T(4,128)(2,1)S(1)}, u32[]{:S(2)}, u32[]{:S(2)}) async-start(bf16[4,128,1152]{2,0,1:T(4,128)(2,1)} %copy.15), calls=%async_computation | async-start | bytes 2359296 | tf_op jit(solution)/shard_map/all_to_all | solution.py:194
  72.4 2.6 %collective-permute-start = (bf16[1152,384]{1,0:T(8,128)(2,1)}, bf16[1152,384]{1,0:T(8,128)(2,1)S(1)}, u32[]{:S(2)}, u32[]{:S(2)}) collective-permute-start(bf16[1152,384]{1,0:T(8,128)(2,1)} %get-tuple-element.7.mine_ref), channel_id=1, source_target_pairs={{0,1},{1,0},{2,3},{3,2},{4,5},{5,4},{6,7},{7,6},{8,9},{9,8},{10,11... | collective-permute-start | bytes 2654216 | tf_op jit(solution)/shard_map/ppermute | solution.py:198
  75.0 0.9 copy-start
  79.6 9.3 %copy-start.2 = (f32[128]{0:T(128)S(1)}, f32[128]{0:T(128)}, u32[]{:S(2)}) copy-start(f32[128]{0:T(128)} %param.15) | copy-start | bytes 1540
  79.6 9.5 %copy-start.3 = (f32[128]{0:T(128)S(1)}, f32[128]{0:T(128)}, u32[]{:S(2)}) copy-start(f32[128]{0:T(128)} %param.16) | copy-start | bytes 1540
  79.6 9.7 %copy-start.1 = (bf16[128,128]{1,0:T(8,128)(2,1)S(1)}, bf16[128,128]{1,0:T(8,128)(2,1)}, u32[]{:S(2)}) copy-start(bf16[128,128]{1,0:T(8,128)(2,1)} %param.17) | copy-start | bytes 98308
  82.2 28.2 %all-to-all-start.1 = ((bf16[2,128,1152]{2,0,1:T(2,128)(2,1)}), bf16[2,128,1152]{2,0,1:T(2,128)(2,1)S(1)}, u32[]{:S(2)}, u32[]{:S(2)}) async-start(bf16[2,128,1152]{2,0,1:T(2,128)(2,1)} %copy.17), calls=%async_computation.1 | async-start | bytes 1179648 | tf_op jit(solution)/shard_map/all_to_all | solution.py:200

commit v2 on v0

v2 whole, which is shorter than its diff:
```python
import jax
import jax.numpy as jnp
from jax import lax
from jax.experimental import pallas as pl
from jax.experimental.pallas import tpu as pltpu
from jax.sharding import Mesh, PartitionSpec as P

EPS = 1e-05
ROW = ("xh", "zh", "zl")
COL = ("xl", "y", "core")
GROUP = ("y", "zh", "zl", "xh", "xl")
F32, BF16 = jnp.float32, jnp.bfloat16
NT = (((1,), (1,)), ((), ()))
TN = (((0,), (0,)), ((), ()))


def sigmoid(x):
    return 0.5 * jnp.tanh(0.5 * x) + 0.5


def layer_norm(x, gain, bias, axis):
    mean = jnp.mean(x, axis=axis, keepdims=True)
    centred = x - mean
    var = jnp.mean(centred * centred, axis=axis, keepdims=True)
    return centred * lax.rsqrt(var + EPS) * gain + bias


def full(*shape):
    return pl.BlockSpec(shape, lambda i: (0,) * len(shape))


def rows_of(place, pair, rows):
    return pl.ds((pair // 2 * 32 + pair % 2) * rows + place, 16, stride=2 * rows)


def project_kernel(pair_ref, mask_ref, gain_ref, bias_ref, w_ref, out_ref, wt_ref, wide_ref):
    step = pl.program_id(0)

    @pl.when(step == 0)
    def _():
        wt_ref[...] = w_ref[...].astype(F32).T.astype(BF16)

    lane = lax.broadcasted_iota(jnp.int32, (48, 384), 1)
    row = lax.broadcasted_iota(jnp.int32, (48, 384), 0)
    spread = (lane // 128 * 16 + lane % 16 == row).astype(F32).astype(BF16)
    keeps = jnp.dot(mask_ref[...].astype(F32).astype(BF16), spread, preferred_element_type=F32)
    lane8 = lax.broadcasted_iota(jnp.int32, (8, 384), 1)
    row8 = lax.broadcasted_iota(jnp.int32, (8, 384), 0)
    for part in range(2):
        x = pair_ref[part * 8 : part * 8 + 8].reshape(8, 3, 16, 128).transpose(1, 0, 2, 3).reshape(384, 128)
        normed = layer_norm(x.T, gain_ref[...], bias_ref[...], 0).astype(BF16)
        keep = jnp.where(lane8 // 16 % 8 == row8, keeps[part * 8 : part * 8 + 8], 0.0)
        keep = jnp.sum(keep, axis=0, keepdims=True)
        for side in range(2):
            gate = jnp.dot(wt_ref[side * 256 : side * 256 + 128, :], normed, preferred_element_type=F32)
            value = jnp.dot(wt_ref[side * 256 + 128 : side * 256 + 256, :], normed, preferred_element_type=F32)
            out = keep * sigmoid(gate) * value
            for kk_hi in range(3):
                at = side * 18 + step * 6 + part * 3 + kk_hi
                wide_ref[pl.ds(at, 128, stride=36), :] = out[:, kk_hi * 128 : kk_hi * 128 + 128]

    @pl.when(step == 2)
    def _():
        out_ref[...] = wide_ref[...].astype(BF16)


def project(pair, mask, gain, bias, w_proj):
    return pl.pallas_call(
        project_kernel,
        grid=(3,),
        out_shape=jax.ShapeDtypeStruct((4608, 128), BF16),
        in_specs=[
            pl.BlockSpec((16, 48, 128), lambda i: (i, 0, 0)),
            pl.BlockSpec((16, 48), lambda i: (i, 0)),
            full(128, 1),
            full(128, 1),
            full(128, 512),
        ],
        out_specs=full(4608, 128),
        scratch_shapes=[pltpu.VMEM((512, 128), BF16), pltpu.VMEM((4608, 128), F32)],
        compiler_params=pltpu.CompilerParams(vmem_limit_bytes=32 << 20),
        name="project",
    )(pair, mask, gain, bias, w_proj)


def gather_kernel(core_ref, recv_ref, swap_ref, send_ref, keep_ref, wide_ref, x_ref, right_ref):
    wide_ref[...] = recv_ref[...].astype(F32)
    for s in range(36):
        for c in range(8):
            x_ref[s * 16 : s * 16 + 16, c * 128 : c * 128 + 128] = wide_ref[rows_of(s, c, 36), :].astype(BF16)
    for n in range(4):
        y = jnp.dot(x_ref[...], swap_ref[:, n * 256 : n * 256 + 256], preferred_element_type=F32).astype(BF16)
        for half in range(2):
            for s in range(36):
                dst = send_ref if s < 18 else right_ref
                at = (s % 18 // 3 * 8 + 2 * n + half) * 16
                lanes = slice(s % 3 * 128, s % 3 * 128 + 128)
                dst[at : at + 16, lanes] = y[s * 16 : s * 16 + 16, half * 128 : half * 128 + 128]
    row = lax.broadcasted_iota(jnp.int32, (128, 256), 0)
    lane = lax.broadcasted_iota(jnp.int32, (128, 256), 1)
    b = row // 16
    for mine in range(2):
        core = core_ref[0] if mine else 1 - core_ref[0]
        pick = (lane // 16 == row % 16) & (lane % 16 == b // 2 * 4 + core * 2 + b % 2)
        pick = pick.astype(F32).astype(BF16)
        for jj_hi in range(3):
            rows = jnp.dot(pick, right_ref[jj_hi * 256 : jj_hi * 256 + 256, :], preferred_element_type=F32).astype(BF16)
            if mine:
                keep_ref[jj_hi * 128 : jj_hi * 128 + 128, :] = rows
            else:
                send_ref[768 + jj_hi * 128 : 768 + jj_hi * 128 + 128, :] = rows


def gather(core, recv, swap):
    vmem = pl.BlockSpec(memory_space=pltpu.VMEM)
    return pl.pallas_call(
        gather_kernel,
        out_shape=(jax.ShapeDtypeStruct((1152, 384), BF16), jax.ShapeDtypeStruct((384, 384), BF16)),
        in_specs=[pl.BlockSpec(memory_space=pltpu.SMEM), vmem, vmem],
        out_specs=(vmem, vmem),
        scratch_shapes=[pltpu.VMEM((4608, 128), F32), pltpu.VMEM((576, 1024), BF16), pltpu.VMEM((768, 384), BF16)],
        compiler_params=pltpu.CompilerParams(vmem_limit_bytes=32 << 20),
        name="gather",
    )(core, recv, swap)


def contract_kernel(mine_ref, other_ref, keep_ref, swap_ref, out_ref, x_ref, wide_ref):
    for i in range(6):
        rows = slice(i * 128, i * 128 + 128)
        mixed = lax.dot_general(mine_ref[rows, :], keep_ref[...], NT, preferred_element_type=F32)
        mixed += lax.dot_general(other_ref[rows, :], other_ref[768:, :], NT, preferred_element_type=F32)
        mixed = mixed.astype(BF16)
        for j in range(3):
            for a in range(8):
                at = (i * 3 + j) * 16
                x_ref[at : at + 16, a * 128 : a * 128 + 128] = mixed[a * 16 : a * 16 + 16, j * 128 : j * 128 + 128]
    for n in range(4):
        y = jnp.dot(x_ref[...], swap_ref[:, n * 256 : n * 256 + 256], preferred_element_type=F32)
        for half in range(2):
            for s in range(18):
                wide_ref[rows_of(s, 2 * n + half, 18), :] = y[s * 16 : s * 16 + 16, half * 128 : half * 128 + 128]
    out_ref[...] = wide_ref[...].astype(BF16)


def contract(mine, other, keep, swap):
    return pl.pallas_call(
        contract_kernel,
        out_shape=jax.ShapeDtypeStruct((2304, 128), BF16),
        scratch_shapes=[pltpu.VMEM((288, 1024), BF16), pltpu.VMEM((2304, 128), F32)],
        compiler_params=pltpu.CompilerParams(vmem_limit_bytes=32 << 20),
        name="contract",
    )(mine, other, keep, swap)


def gate_kernel(pair_ref, gain_ref, bias_ref, w_ref, out_ref):
    x = pair_ref[...].reshape(16 * 48, 128)
    normed = layer_norm(x, gain_ref[...], bias_ref[...], -1).astype(BF16)
    gate = sigmoid(jnp.dot(normed, w_ref[...], preferred_element_type=F32))
    out_ref[...] = gate.reshape(16, 48, 128)


def gating(pair, gain, bias, w_gate):
    return pl.pallas_call(
        gate_kernel,
        grid=(3,),
        out_shape=jax.ShapeDtypeStruct((48, 48, 128), F32),
        in_specs=[pl.BlockSpec((16, 48, 128), lambda i: (i, 0, 0)), full(1, 128), full(1, 128), full(128, 128)],
        out_specs=pl.BlockSpec((16, 48, 128), lambda i: (i, 0, 0)),
        cost_estimate=pl.CostEstimate(flops=75_000_000, bytes_accessed=2_400_000, transcendentals=300_000),
        compiler_params=pltpu.CompilerParams(vmem_limit_bytes=32 << 20),
        name="gate",
    )(pair, gain, bias, w_gate)


def finish_kernel(mixed_ref, gate_ref, gain_ref, bias_ref, w_ref, out_ref, wide_ref):
    step = pl.program_id(0)

    @pl.when(step == 0)
    def _():
        wide_ref[...] = mixed_ref[...].astype(F32)

    for part in range(2):
        at = step * 6 + part * 3
        for jj_hi in range(3):
            mixed = wide_ref[pl.ds(at + jj_hi, 128, stride=18), :]
            normed = layer_norm(mixed, gain_ref[...], bias_ref[...], 0).astype(BF16)
            projected = lax.dot_general(normed, w_ref[...], TN, preferred_element_type=F32).reshape(8, 16, 128)
            rows, cols = slice(part * 8, part * 8 + 8), slice(jj_hi * 16, jj_hi * 16 + 16)
            out_ref[rows, cols, :] = gate_ref[rows, cols, :] * projected


def finish(mixed, gate, gain, bias, w_out):
    return pl.pallas_call(
        finish_kernel,
        grid=(3,),
        out_shape=jax.ShapeDtypeStruct((48, 48, 128), F32),
        in_specs=[
            full(2304, 128),
            pl.BlockSpec((16, 48, 128), lambda i: (i, 0, 0)),
            full(128, 1),
            full(128, 1),
            full(128, 128),
        ],
        out_specs=pl.BlockSpec((16, 48, 128), lambda i: (i, 0, 0)),
        scratch_shapes=[pltpu.VMEM((2304, 128), F32)],
        compiler_params=pltpu.CompilerParams(vmem_limit_bytes=32 << 20),
        name="finish",
    )(mixed, gate, gain, bias, w_out)


def exchange(messages):
    rows = messages.shape[0] // 128
    tiles = messages.reshape(128, 9, rows // 9, 128)
    return lax.all_to_all(tiles, GROUP, 0, 0, tiled=True).reshape(128 * rows, 128)


def per_device(pair, pair_mask, ln_gain, ln_bias, w_proj, w_gate, out_gain, out_bias, w_out):
    recv = exchange(project(pair, pair_mask, ln_gain.reshape(128, 1), ln_bias.reshape(128, 1), w_proj))
    gate = gating(pair, ln_gain.reshape(1, 128), ln_bias.reshape(1, 128), w_gate)
    place = jnp.arange(1024)
    target = place // 16 % 8 * 128 + place // 128 * 16 + place % 16
    swap = (target[:, None] == place[None, :]).astype(BF16)
    core = lax.axis_index("core").astype(jnp.int32).reshape(1)
    mine, keep = gather(core, recv, swap)
    other = lax.ppermute(mine, "core", [(0, 1), (1, 0)])
    mixed = exchange(contract(mine, other, keep, swap))
    return finish(mixed, gate, out_gain.reshape(128, 1), out_bias.reshape(128, 1), w_out)


def solution(mesh):
    fine = Mesh(mesh.devices.reshape(2, 4, 2, 2, 4, 2), ROW + COL)
    return jax.shard_map(
        per_device,
        mesh=fine,
        in_specs=(P(ROW, COL, None), P(ROW, COL), P(), P(), P(), P(), P(), P(), P()),
        out_specs=P(ROW, COL, None),
        check_vma=False,
    )
```

time: 390 us -> 93.5 us (0.24)
  the two profiles are of different devices: /device:TPU:19 before, /device:TPU:32 now
where the time goes in v2:
time: 93.5 us; the launch traced here: 93.1 us
  waiting for transfers between devices  54.1 us (58%)
  starting transfers between devices  22.4 us (24%)
  Pallas kernels  11.5 us (12%)
  local copies, waits for them, and re-layouts  4.68 us (5%)
    all_to_all x2, waiting for transfers between devices, exchange(): lax.all_to_all(tiles, GROUP, 0, 0, tiled=True).reshape(128 * rows, 128)  51.6 us
    all_to_all x2, starting transfers between devices, exchange(): lax.all_to_all(tiles, GROUP, 0, 0, tiled=True).reshape(128 * rows, 128)  22.3 us
    pallas_call x1, Pallas kernels, project(): pl.pallas_call(project_kernel, grid=(3,), out_shape=jax.ShapeDtypeStruct(...  2.98 us
    unnamed x20, local copies, waits for them, and re-layouts  2.94 us
    pallas_call x1, Pallas kernels, contract(): pl.pallas_call(contract_kernel, out_shape=jax.ShapeDtypeStruct((2304, 128...  2.79 us
    pallas_call x1, Pallas kernels, finish(): pl.pallas_call(finish_kernel, grid=(3,), out_shape=jax.ShapeDtypeStruct((...  2.59 us
    ppermute x1, waiting for transfers between devices, per_device(): other = lax.ppermute(mine, 'core', [(0, 1), (1, 0)])  2.41 us
  transfers between devices with their start and end apart: 3, of which 3 were waited for; matrix products, arithmetic and copies ran while one was open for 1% of the time, Pallas kernels for 1%

profile of v2, /device:TPU:32, one launch (start us, length us, event | category | flops | bytes accessed | tf_op | source)
XLA Modules:
  0.0 93.1 jit_solution(16613331772702841792)
XLA Ops:
  0.0 0.8 copy.10.gain_ref
  0.8 0.8 copy.11.bias_ref
  1.5 0.0 copy-start
  1.5 1.3 %copy-done = f32[48,48,128]{2,1,0:T(8,128)S(1)} copy-done((f32[48,48,128]{2,1,0:T(8,128)S(1)}, f32[48,48,128]{2,1,0:T(8,128)}, u32[]{:S(2)}) %copy-start) | copy-done | bytes 1179672
  2.8 0.0 copy-start.2
  2.8 0.9 copy-done.2
  3.7 0.0 copy-start.5
  3.7 0.7 copy-done.5
  4.4 3.0 %project.1 = bf16[4608,128]{1,0:T(8,128)(2,1)} custom-call(f32[48,48,128]{2,1,0:T(8,128)S(1)} %copy-done, s32[48,48]{1,0:T(8,128)S(1)} %copy-done.5, f32[128,1]{1,0:T(8,128)S(1)} %copy.10.gain_ref, f32[128,1]{1,0:T(8,128)S(1)} %copy.11.bias_ref, bf16[128,512]{1,0:T(8,128)(2,1)S(1)} %copy-done.2), custom_call_target="tpu_custom_call" | custom-call | tf_op jit(solution)/shard_map/project/pallas_call | solution.py:68
  7.4 15.0 %all-to-all-start = ((bf16[128,9,4,128]{3,2,1,0:T(4,128)(2,1)}), bf16[128,9,4,128]{3,2,1,0:T(4,128)(2,1)S(1)}, u32[]{:S(2)}, u32[]{:S(2)}) async-start(bf16[128,9,4,128]{3,2,1,0:T(4,128)(2,1)} %bitcast.3), calls=%async_computation | async-start | bytes 2359296 | tf_op jit(solution)/shard_map/all_to_all | solution.py:214
  22.4 0.4 fusion.swap_ref
  22.9 32.4 %all-to-all-done = bf16[128,9,4,128]{3,2,1,0:T(4,128)(2,1)S(1)} async-done(((bf16[128,9,4,128]{3,2,1,0:T(4,128)(2,1)}), bf16[128,9,4,128]{3,2,1,0:T(4,128)(2,1)S(1)}, u32[]{:S(2)}, u32[]{:S(2)}) %all-to-all-start) | async-done | bytes 1179680 | tf_op jit(solution)/shard_map/all_to_all | solution.py:214
  55.2 1.8 %gather.1 = (bf16[1152,384]{1,0:T(8,128)(2,1)S(1)}, bf16[384,384]{1,0:T(8,128)(2,1)S(1)}) custom-call(s32[1]{0:T(128)} %bitcast.core_ref, bf16[4608,128]{1,0:T(8,128)(2,1)S(1)} %bitcast.11, bf16[1024,1024]{1,0:T(8,128)(2,1)S(1)} %fusion.swap_ref), custom_call_target="tpu_custom_call" | custom-call | tf_op jit(solution)/shard_map/gather/pallas_call | solution.py:116
  57.1 0.1 collective-permute-start
  57.2 2.4 %collective-permute-done.other_ref = bf16[1152,384]{1,0:T(8,128)(2,1)S(1)} collective-permute-done((bf16[1152,384]{1,0:T(8,128)(2,1)S(1)}, bf16[1152,384]{1,0:T(8,128)(2,1)S(1)}, u32[]{:S(2)}, u32[]{:S(2)}) %collective-permute-start) | collective-permute-done | bytes 884768 | tf_op jit(solution)/shard_map/ppermute | solution.py:225
  59.6 0.0 copy-start.8
  59.6 2.8 %contract.1 = bf16[2304,128]{1,0:T(8,128)(2,1)} custom-call(bf16[1152,384]{1,0:T(8,128)(2,1)S(1)} %get-tuple-element.7.mine_ref, bf16[1152,384]{1,0:T(8,128)(2,1)S(1)} %collective-permute-done.other_ref, bf16[384,384]{1,0:T(8,128)(2,1)S(1)} %get-tuple-element.8.keep_ref, bf16[1024,1024]{1,0:T(8,128)(2,1)S(1)} %fusion.swap_ref), custom_call_target="tpu_custom_call" | custom-call | tf_op jit(solution)/shard_map/contract/pallas_call | solution.py:146
  62.4 0.0 copy-start.9
  62.4 0.0 copy-start.1
  62.4 0.0 copy-start.3
  62.4 0.0 copy-start.6
  62.4 0.0 copy-start.7
  62.4 7.3 %all-to-all-start.1 = ((bf16[128,9,2,128]{3,2,1,0:T(2,128)(2,1)}), bf16[128,9,2,128]{3,2,1,0:T(2,128)(2,1)S(1)}, u32[]{:S(2)}, u32[]{:S(2)}) async-start(bf16[128,9,2,128]{3,2,1,0:T(2,128)(2,1)} %bitcast.5), calls=%async_computation.1 | async-start | bytes 1179648 | tf_op jit(solution)/shard_map/all_to_all | solution.py:214
  69.7 0.0 copy-done.8
  69.7 0.1 copy.12.gain_ref
  69.8 0.0 copy-done.9
  69.8 0.1 copy.13.bias_ref
  69.9 0.0 copy-done.1
  70.0 0.0 copy-done.3
  70.0 0.0 copy-done.6
  70.0 0.0 copy-done.7
  70.0 0.0 copy-start.4
  70.0 1.3 %gate.1.gate_ref = f32[48,48,128]{2,1,0:T(8,128)S(1)} custom-call(f32[48,48,128]{2,1,0:T(8,128)S(1)} %copy-done.1, f32[1,128]{1,0:T(1,128)S(1)} %bitcast.14, f32[1,128]{1,0:T(1,128)S(1)} %bitcast.16, bf16[128,128]{1,0:T(8,128)(2,1)S(1)} %copy-done.3), custom_call_target="tpu_custom_call" | custom-call | flops 75000000 | bytes 2400000 | tf_op jit(solution)/shard_map/gate/pallas_call | solution.py:163
  71.3 19.3 %all-to-all-done.1 = bf16[128,9,2,128]{3,2,1,0:T(2,128)(2,1)S(1)} async-done(((bf16[128,9,2,128]{3,2,1,0:T(2,128)(2,1)}), bf16[128,9,2,128]{3,2,1,0:T(2,128)(2,1)S(1)}, u32[]{:S(2)}, u32[]{:S(2)}) %all-to-all-start.1) | async-done | bytes 589856 | tf_op jit(solution)/shard_map/all_to_all | solution.py:214
  90.5 0.0 copy-done.4
  90.5 2.6 %finish.1 = f32[48,48,128]{2,1,0:T(8,128)} custom-call(bf16[2304,128]{1,0:T(8,128)(2,1)S(1)} %bitcast.12, f32[48,48,128]{2,1,0:T(8,128)S(1)} %gate.1.gate_ref, f32[128,1]{1,0:T(8,128)S(1)} %copy.12.gain_ref, f32[128,1]{1,0:T(8,128)S(1)} %copy.13.bias_ref, bf16[128,128]{1,0:T(8,128)(2,1)S(1)} %copy-done.4), custom_call_target="tpu_custom_call" | custom-call | tf_op jit(solution)/shard_map/finish/pallas_call | solution.py:193
  (1 shorter events, 0.0 us)
Async XLA Ops:
  1.5 1.3 %copy-start = (f32[48,48,128]{2,1,0:T(8,128)S(1)}, f32[48,48,128]{2,1,0:T(8,128)}, u32[]{:S(2)}) copy-start(f32[48,48,128]{2,1,0:T(8,128)} %pair_ref.3) | copy-start | bytes 3538948
  2.8 0.9 copy-start.2
  3.7 0.7 copy-start.5
  7.4 47.8 %all-to-all-start = ((bf16[128,9,4,128]{3,2,1,0:T(4,128)(2,1)}), bf16[128,9,4,128]{3,2,1,0:T(4,128)(2,1)S(1)}, u32[]{:S(2)}, u32[]{:S(2)}) async-start(bf16[128,9,4,128]{3,2,1,0:T(4,128)(2,1)} %bitcast.3), calls=%async_computation | async-start | bytes 2359296 | tf_op jit(solution)/shard_map/all_to_all | solution.py:214
  57.1 2.5 %collective-permute-start = (bf16[1152,384]{1,0:T(8,128)(2,1)S(1)}, bf16[1152,384]{1,0:T(8,128)(2,1)S(1)}, u32[]{:S(2)}, u32[]{:S(2)}) collective-permute-start(bf16[1152,384]{1,0:T(8,128)(2,1)S(1)} %get-tuple-element.7.mine_ref), channel_id=1, source_target_pairs={{0,1},{1,0},{2,3},{3,2},{4,5},{5,4},{6,7},{7,6},{8,9},{9,8},{10,11... | collective-permute-start | bytes 2654216 | tf_op jit(solution)/shard_map/ppermute | solution.py:225
  59.6 10.1 %copy-start.8 = (f32[128]{0:T(128)S(1)}, f32[128]{0:T(128)}, u32[]{:S(2)}) copy-start(f32[128]{0:T(128)} %param.15) | copy-start | bytes 1540
  62.4 7.5 %copy-start.9 = (f32[128]{0:T(128)S(1)}, f32[128]{0:T(128)}, u32[]{:S(2)}) copy-start(f32[128]{0:T(128)} %param.16) | copy-start | bytes 1540
  62.4 7.6 %copy-start.1 = (f32[48,48,128]{2,1,0:T(8,128)S(1)}, f32[48,48,128]{2,1,0:T(8,128)}, u32[]{:S(2)}) copy-start(f32[48,48,128]{2,1,0:T(8,128)} %pair_ref.3) | copy-start | bytes 3538948
  62.4 7.6 %copy-start.3 = (bf16[128,128]{1,0:T(8,128)(2,1)S(1)}, bf16[128,128]{1,0:T(8,128)(2,1)}, u32[]{:S(2)}) copy-start(bf16[128,128]{1,0:T(8,128)(2,1)} %w_ref.4) | copy-start | bytes 98308
  62.4 7.6 %copy-start.6 = (f32[128]{0:T(128)S(1)}, f32[128]{0:T(128)}, u32[]{:S(2)}) copy-start(f32[128]{0:T(128)} %param.11) | copy-start | bytes 1540
  62.4 7.6 %copy-start.7 = (f32[128]{0:T(128)S(1)}, f32[128]{0:T(128)}, u32[]{:S(2)}) copy-start(f32[128]{0:T(128)} %param.12) | copy-start | bytes 1540
  62.4 28.1 %all-to-all-start.1 = ((bf16[128,9,2,128]{3,2,1,0:T(2,128)(2,1)}), bf16[128,9,2,128]{3,2,1,0:T(2,128)(2,1)S(1)}, u32[]{:S(2)}, u32[]{:S(2)}) async-start(bf16[128,9,2,128]{3,2,1,0:T(2,128)(2,1)} %bitcast.5), calls=%async_computation.1 | async-start | bytes 1179648 | tf_op jit(solution)/shard_map/all_to_all | solution.py:214
  70.0 20.6 %copy-start.4 = (bf16[128,128]{1,0:T(8,128)(2,1)S(1)}, bf16[128,128]{1,0:T(8,128)(2,1)}, u32[]{:S(2)}) copy-start(bf16[128,128]{1,0:T(8,128)(2,1)} %w_ref.5) | copy-start | bytes 98308

commit v3 on v2

--- a/solution.py
+++ b/solution.py
@@ -25,6 +25,10 @@
     return centred * lax.rsqrt(var + EPS) * gain + bias
 
 
+def column(row):
+    return jnp.broadcast_to(row, (8, 128)).T[:, :1]
+
+
 def full(*shape):
     return pl.BlockSpec(shape, lambda i: (0,) * len(shape))
 
@@ -46,9 +50,10 @@
     keeps = jnp.dot(mask_ref[...].astype(F32).astype(BF16), spread, preferred_element_type=F32)
     lane8 = lax.broadcasted_iota(jnp.int32, (8, 384), 1)
     row8 = lax.broadcasted_iota(jnp.int32, (8, 384), 0)
+    gain, bias = column(gain_ref[...]), column(bias_ref[...])
     for part in range(2):
         x = pair_ref[part * 8 : part * 8 + 8].reshape(8, 3, 16, 128).transpose(1, 0, 2, 3).reshape(384, 128)
-        normed = layer_norm(x.T, gain_ref[...], bias_ref[...], 0).astype(BF16)
+        normed = layer_norm(x.T, gain, bias, 0).astype(BF16)
         keep = jnp.where(lane8 // 16 % 8 == row8, keeps[part * 8 : part * 8 + 8], 0.0)
         keep = jnp.sum(keep, axis=0, keepdims=True)
         for side in range(2):
@@ -72,13 +77,13 @@
         in_specs=[
             pl.BlockSpec((16, 48, 128), lambda i: (i, 0, 0)),
             pl.BlockSpec((16, 48), lambda i: (i, 0)),
-            full(128, 1),
-            full(128, 1),
+            full(1, 128),
+            full(1, 128),
             full(128, 512),
         ],
         out_specs=full(4608, 128),
         scratch_shapes=[pltpu.VMEM((512, 128), BF16), pltpu.VMEM((4608, 128), F32)],
-        compiler_params=pltpu.CompilerParams(vmem_limit_bytes=32 << 20),
+        compiler_params=pltpu.CompilerParams(vmem_limit_bytes=60 << 20),
         name="project",
     )(pair, mask, gain, bias, w_proj)
 
@@ -179,11 +184,12 @@
     def _():
         wide_ref[...] = mixed_ref[...].astype(F32)
 
+    gain, bias = column(gain_ref[...]), column(bias_ref[...])
     for part in range(2):
         at = step * 6 + part * 3
         for jj_hi in range(3):
             mixed = wide_ref[pl.ds(at + jj_hi, 128, stride=18), :]
-            normed = layer_norm(mixed, gain_ref[...], bias_ref[...], 0).astype(BF16)
+            normed = layer_norm(mixed, gain, bias, 0).astype(BF16)
             projected = lax.dot_general(normed, w_ref[...], TN, preferred_element_type=F32).reshape(8, 16, 128)
             rows, cols = slice(part * 8, part * 8 + 8), slice(jj_hi * 16, jj_hi * 16 + 16)
             out_ref[rows, cols, :] = gate_ref[rows, cols, :] * projected
@@ -197,8 +203,8 @@
         in_specs=[
             full(2304, 128),
             pl.BlockSpec((16, 48, 128), lambda i: (i, 0, 0)),
-            full(128, 1),
-            full(128, 1),
+            full(1, 128),
+            full(1, 128),
             full(128, 128),
         ],
         out_specs=pl.BlockSpec((16, 48, 128), lambda i: (i, 0, 0)),
@@ -215,7 +221,7 @@
 
 
 def per_device(pair, pair_mask, ln_gain, ln_bias, w_proj, w_gate, out_gain, out_bias, w_out):
-    recv = exchange(project(pair, pair_mask, ln_gain.reshape(128, 1), ln_bias.reshape(128, 1), w_proj))
+    recv = exchange(project(pair, pair_mask, ln_gain.reshape(1, 128), ln_bias.reshape(1, 128), w_proj))
     gate = gating(pair, ln_gain.reshape(1, 128), ln_bias.reshape(1, 128), w_gate)
     place = jnp.arange(1024)
     target = place // 16 % 8 * 128 + place // 128 * 16 + place % 16
@@ -224,7 +230,7 @@
     mine, keep = gather(core, recv, swap)
     other = lax.ppermute(mine, "core", [(0, 1), (1, 0)])
     mixed = exchange(contract(mine, other, keep, swap))
-    return finish(mixed, gate, out_gain.reshape(128, 1), out_bias.reshape(128, 1), w_out)
+    return finish(mixed, gate, out_gain.reshape(1, 128), out_bias.reshape(1, 128), w_out)
 
 
 def solution(mesh):

time: 93.5 us -> 90.7 us (0.970)
  local copies, waits for them, and re-layouts: 4.68 us -> 0.03 us
  Pallas kernels: 11.5 us -> 13.2 us
    unnamed x20 -> x14, local copies, waits for them, and re-layouts: 2.94 us -> 0.03 us
    pallas_call x1, Pallas kernels: 2.98 us -> 4.75 us  [project(): pl.pallas_call(project_kernel, grid=(3,), out_shape=jax.ShapeDtypeStruct(...]
    reshape x4 -> x0, local copies, waits for them, and re-layouts: 1.75 us -> none  [the longest x1 0.76 us: per_device(): ln_gain.reshape(128, 1)]
  transfers between devices with their start and end apart: 3 -> 3, of which waited for: 3 -> 3; matrix products, arithmetic and copies ran while one was open for 1% -> 0% of each run, Pallas kernels for 1% -> 1%
where the time goes in v3:
time: 90.7 us; the launch traced here: 90.4 us
  waiting for transfers between devices  54.3 us (60%)
  starting transfers between devices  22.4 us (25%)
  Pallas kernels  13.2 us (15%)
    all_to_all x2, waiting for transfers between devices, exchange(): lax.all_to_all(tiles, GROUP, 0, 0, tiled=True).reshape(128 * rows, 128)  51.9 us
    all_to_all x2, starting transfers between devices, exchange(): lax.all_to_all(tiles, GROUP, 0, 0, tiled=True).reshape(128 * rows, 128)  22.3 us
    pallas_call x1, Pallas kernels, project(): pl.pallas_call(project_kernel, grid=(3,), out_shape=jax.ShapeDtypeStruct(...  4.75 us
    pallas_call x1, Pallas kernels, contract(): pl.pallas_call(contract_kernel, out_shape=jax.ShapeDtypeStruct((2304, 128...  2.78 us
    pallas_call x1, Pallas kernels, finish(): pl.pallas_call(finish_kernel, grid=(3,), out_shape=jax.ShapeDtypeStruct((...  2.59 us
    ppermute x1, waiting for transfers between devices, per_device(): other = lax.ppermute(mine, 'core', [(0, 1), (1, 0)])  2.41 us
    pallas_call x1, Pallas kernels, gather(): pl.pallas_call(gather_kernel, out_shape=(jax.ShapeDtypeStruct((1152, 384)...  1.82 us
  transfers between devices with their start and end apart: 3, of which 3 were waited for; matrix products, arithmetic and copies ran while one was open for 0% of the time, Pallas kernels for 1%

profile of v3, /device:TPU:32, one launch (start us, length us, event | category | flops | bytes accessed | tf_op | source)
XLA Modules:
  0.0 90.4 jit_solution(8091080612033618783)
XLA Ops:
  0.0 4.8 %project.1 = bf16[4608,128]{1,0:T(8,128)(2,1)} custom-call(f32[48,48,128]{2,1,0:T(8,128)} %pair_ref.3, s32[48,48]{1,0:T(8,128)} %mask_ref.1, f32[1,128]{1,0:T(1,128)} %bitcast.11, f32[1,128]{1,0:T(1,128)} %bitcast.13, bf16[128,512]{1,0:T(8,128)(2,1)} %w_ref.3), custom_call_target="tpu_custom_call" | custom-call | tf_op jit(solution)/shard_map/project/pallas_call | solution.py:73
  4.8 15.0 %all-to-all-start = ((bf16[128,9,4,128]{3,2,1,0:T(4,128)(2,1)}), bf16[128,9,4,128]{3,2,1,0:T(4,128)(2,1)S(1)}, u32[]{:S(2)}, u32[]{:S(2)}) async-start(bf16[128,9,4,128]{3,2,1,0:T(4,128)(2,1)} %bitcast.17), calls=%async_computation | async-start | bytes 2359296 | tf_op jit(solution)/shard_map/all_to_all | solution.py:220
  19.8 0.4 fusion.swap_ref
  20.2 32.4 %all-to-all-done = bf16[128,9,4,128]{3,2,1,0:T(4,128)(2,1)S(1)} async-done(((bf16[128,9,4,128]{3,2,1,0:T(4,128)(2,1)}), bf16[128,9,4,128]{3,2,1,0:T(4,128)(2,1)S(1)}, u32[]{:S(2)}, u32[]{:S(2)}) %all-to-all-start) | async-done | bytes 1179680 | tf_op jit(solution)/shard_map/all_to_all | solution.py:220
  52.6 1.8 %gather.1 = (bf16[1152,384]{1,0:T(8,128)(2,1)S(1)}, bf16[384,384]{1,0:T(8,128)(2,1)S(1)}) custom-call(s32[1]{0:T(128)} %bitcast.core_ref, bf16[4608,128]{1,0:T(8,128)(2,1)S(1)} %bitcast.9, bf16[1024,1024]{1,0:T(8,128)(2,1)S(1)} %fusion.swap_ref), custom_call_target="tpu_custom_call" | custom-call | tf_op jit(solution)/shard_map/gather/pallas_call | solution.py:121
  54.4 0.1 collective-permute-start
  54.5 2.4 %collective-permute-done.other_ref = bf16[1152,384]{1,0:T(8,128)(2,1)S(1)} collective-permute-done((bf16[1152,384]{1,0:T(8,128)(2,1)S(1)}, bf16[1152,384]{1,0:T(8,128)(2,1)S(1)}, u32[]{:S(2)}, u32[]{:S(2)}) %collective-permute-start) | collective-permute-done | bytes 884768 | tf_op jit(solution)/shard_map/ppermute | solution.py:231
  56.9 0.0 copy-start.1
  56.9 2.8 %contract.1 = bf16[2304,128]{1,0:T(8,128)(2,1)} custom-call(bf16[1152,384]{1,0:T(8,128)(2,1)S(1)} %get-tuple-element.7.mine_ref, bf16[1152,384]{1,0:T(8,128)(2,1)S(1)} %collective-permute-done.other_ref, bf16[384,384]{1,0:T(8,128)(2,1)S(1)} %get-tuple-element.8.keep_ref, bf16[1024,1024]{1,0:T(8,128)(2,1)S(1)} %fusion.swap_ref), custom_call_target="tpu_custom_call" | custom-call | tf_op jit(solution)/shard_map/contract/pallas_call | solution.py:151
  59.7 0.0 copy-start
  59.7 0.0 copy-start.3
  59.7 0.0 copy-start.4
  59.7 7.3 %all-to-all-start.1 = ((bf16[128,9,2,128]{3,2,1,0:T(2,128)(2,1)}), bf16[128,9,2,128]{3,2,1,0:T(2,128)(2,1)S(1)}, u32[]{:S(2)}, u32[]{:S(2)}) async-start(bf16[128,9,2,128]{3,2,1,0:T(2,128)(2,1)} %bitcast.5), calls=%async_computation.1 | async-start | bytes 1179648 | tf_op jit(solution)/shard_map/all_to_all | solution.py:220
  67.0 0.0 copy-done.1
  67.0 0.0 copy-done
  67.0 0.0 copy-done.3
  67.0 0.0 copy-done.4
  67.1 0.0 copy-start.2
  67.1 0.0 copy-start.5
  67.1 0.0 copy-start.6
  67.1 1.3 %gate.1.gate_ref = f32[48,48,128]{2,1,0:T(8,128)S(1)} custom-call(f32[48,48,128]{2,1,0:T(8,128)S(1)} %copy-done, f32[1,128]{1,0:T(1,128)S(1)} %bitcast.12, f32[1,128]{1,0:T(1,128)S(1)} %bitcast.14, bf16[128,128]{1,0:T(8,128)(2,1)S(1)} %copy-done.1), custom_call_target="tpu_custom_call" | custom-call | flops 75000000 | bytes 2400000 | tf_op jit(solution)/shard_map/gate/pallas_call | solution.py:168
  68.4 19.5 %all-to-all-done.1 = bf16[128,9,2,128]{3,2,1,0:T(2,128)(2,1)S(1)} async-done(((bf16[128,9,2,128]{3,2,1,0:T(2,128)(2,1)}), bf16[128,9,2,128]{3,2,1,0:T(2,128)(2,1)S(1)}, u32[]{:S(2)}, u32[]{:S(2)}) %all-to-all-start.1) | async-done | bytes 589856 | tf_op jit(solution)/shard_map/all_to_all | solution.py:220
  87.8 0.0 copy-done.2
  87.8 0.0 copy-done.5
  87.9 0.0 copy-done.6
  87.9 2.6 %finish.1 = f32[48,48,128]{2,1,0:T(8,128)} custom-call(bf16[2304,128]{1,0:T(8,128)(2,1)S(1)} %bitcast.10, f32[48,48,128]{2,1,0:T(8,128)S(1)} %gate.1.gate_ref, f32[1,128]{1,0:T(1,128)S(1)} %bitcast.15, f32[1,128]{1,0:T(1,128)S(1)} %bitcast.16, bf16[128,128]{1,0:T(8,128)(2,1)S(1)} %copy-done.2), custom_call_target="tpu_custom_call" | custom-call | tf_op jit(solution)/shard_map/finish/pallas_call | solution.py:199
  (1 shorter events, 0.0 us)
Async XLA Ops:
  4.8 47.8 %all-to-all-start = ((bf16[128,9,4,128]{3,2,1,0:T(4,128)(2,1)}), bf16[128,9,4,128]{3,2,1,0:T(4,128)(2,1)S(1)}, u32[]{:S(2)}, u32[]{:S(2)}) async-start(bf16[128,9,4,128]{3,2,1,0:T(4,128)(2,1)} %bitcast.17), calls=%async_computation | async-start | bytes 2359296 | tf_op jit(solution)/shard_map/all_to_all | solution.py:220
  54.4 2.5 %collective-permute-start = (bf16[1152,384]{1,0:T(8,128)(2,1)S(1)}, bf16[1152,384]{1,0:T(8,128)(2,1)S(1)}, u32[]{:S(2)}, u32[]{:S(2)}) collective-permute-start(bf16[1152,384]{1,0:T(8,128)(2,1)S(1)} %get-tuple-element.7.mine_ref), channel_id=1, source_target_pairs={{0,1},{1,0},{2,3},{3,2},{4,5},{5,4},{6,7},{7,6},{8,9},{9,8},{10,11... | collective-permute-start | bytes 2654216 | tf_op jit(solution)/shard_map/ppermute | solution.py:231
  56.9 10.1 %copy-start.1 = (bf16[128,128]{1,0:T(8,128)(2,1)S(1)}, bf16[128,128]{1,0:T(8,128)(2,1)}, u32[]{:S(2)}) copy-start(bf16[128,128]{1,0:T(8,128)(2,1)} %w_ref.4) | copy-start | bytes 98308
  59.7 7.3 %copy-start = (f32[48,48,128]{2,1,0:T(8,128)S(1)}, f32[48,48,128]{2,1,0:T(8,128)}, u32[]{:S(2)}) copy-start(f32[48,48,128]{2,1,0:T(8,128)} %pair_ref.3) | copy-start | bytes 3538948
  59.7 7.3 %copy-start.3 = (f32[128]{0:T(128)S(1)}, f32[128]{0:T(128)}, u32[]{:S(2)}) copy-start(f32[128]{0:T(128)} %param.11) | copy-start | bytes 1540
  59.7 7.3 %copy-start.4 = (f32[128]{0:T(128)S(1)}, f32[128]{0:T(128)}, u32[]{:S(2)}) copy-start(f32[128]{0:T(128)} %param.12) | copy-start | bytes 1540
  59.7 28.1 %all-to-all-start.1 = ((bf16[128,9,2,128]{3,2,1,0:T(2,128)(2,1)}), bf16[128,9,2,128]{3,2,1,0:T(2,128)(2,1)S(1)}, u32[]{:S(2)}, u32[]{:S(2)}) async-start(bf16[128,9,2,128]{3,2,1,0:T(2,128)(2,1)} %bitcast.5), calls=%async_computation.1 | async-start | bytes 1179648 | tf_op jit(solution)/shard_map/all_to_all | solution.py:220
  67.1 20.8 %copy-start.2 = (bf16[128,128]{1,0:T(8,128)(2,1)S(1)}, bf16[128,128]{1,0:T(8,128)(2,1)}, u32[]{:S(2)}) copy-start(bf16[128,128]{1,0:T(8,128)(2,1)} %w_ref.5) | copy-start | bytes 98308
  67.1 20.8 %copy-start.5 = (f32[128]{0:T(128)S(1)}, f32[128]{0:T(128)}, u32[]{:S(2)}) copy-start(f32[128]{0:T(128)} %param.15) | copy-start | bytes 1540
  67.1 20.8 %copy-start.6 = (f32[128]{0:T(128)S(1)}, f32[128]{0:T(128)}, u32[]{:S(2)}) copy-start(f32[128]{0:T(128)} %param.16) | copy-start | bytes 1540

commit v4 on v3

--- a/solution.py
+++ b/solution.py
@@ -1,5 +1,6 @@
 import jax
 import jax.numpy as jnp
+import numpy as np
 from jax import lax
 from jax.experimental import pallas as pl
 from jax.experimental.pallas import tpu as pltpu
@@ -37,55 +38,64 @@
     return pl.ds((pair // 2 * 32 + pair % 2) * rows + place, 16, stride=2 * rows)
 
 
-def project_kernel(pair_ref, mask_ref, gain_ref, bias_ref, w_ref, out_ref, wt_ref, wide_ref):
-    step = pl.program_id(0)
-
-    @pl.when(step == 0)
-    def _():
-        wt_ref[...] = w_ref[...].astype(F32).T.astype(BF16)
-
+def project_kernel(
+    pair_hbm, mask_hbm, gain_hbm, bias_hbm, w_hbm, out_ref,
+    pair_ref, mask_ref, gain_ref, bias_ref, w_ref, wt_ref, wide_ref, sems,
+):
+    small = [
+        pltpu.make_async_copy(src, dst, sems.at[6 + n])
+        for n, (src, dst) in enumerate(((w_hbm, w_ref), (gain_hbm, gain_ref), (bias_hbm, bias_ref), (mask_hbm, mask_ref)))
+    ]
+    chunks = [
+        pltpu.make_async_copy(pair_hbm.at[pl.ds(part * 8, 8)], pair_ref.at[pl.ds(part * 8, 8)], sems.at[part])
+        for part in range(6)
+    ]
+    small[0].start()
+    chunks[0].start()
+    for copy in small[1:] + chunks[1:]:
+        copy.start()
     lane = lax.broadcasted_iota(jnp.int32, (48, 384), 1)
     row = lax.broadcasted_iota(jnp.int32, (48, 384), 0)
     spread = (lane // 128 * 16 + lane % 16 == row).astype(F32).astype(BF16)
+    own = lax.broadcasted_iota(jnp.int32, (8, 384), 1) // 16 % 8 == lax.broadcasted_iota(jnp.int32, (8, 384), 0)
+    for copy in small + chunks:
+        copy.wait()
+    wt_ref[...] = w_ref[...].astype(F32).T.astype(BF16)
     keeps = jnp.dot(mask_ref[...].astype(F32).astype(BF16), spread, preferred_element_type=F32)
-    lane8 = lax.broadcasted_iota(jnp.int32, (8, 384), 1)
-    row8 = lax.broadcasted_iota(jnp.int32, (8, 384), 0)
     gain, bias = column(gain_ref[...]), column(bias_ref[...])
-    for part in range(2):
+    for part in range(6):
         x = pair_ref[part * 8 : part * 8 + 8].reshape(8, 3, 16, 128).transpose(1, 0, 2, 3).reshape(384, 128)
         normed = layer_norm(x.T, gain, bias, 0).astype(BF16)
-        keep = jnp.where(lane8 // 16 % 8 == row8, keeps[part * 8 : part * 8 + 8], 0.0)
-        keep = jnp.sum(keep, axis=0, keepdims=True)
+        keep = jnp.sum(jnp.where(own, keeps[part * 8 : part * 8 + 8], 0.0), axis=0, keepdims=True)
         for side in range(2):
             gate = jnp.dot(wt_ref[side * 256 : side * 256 + 128, :], normed, preferred_element_type=F32)
             value = jnp.dot(wt_ref[side * 256 + 128 : side * 256 + 256, :], normed, preferred_element_type=F32)
             out = keep * sigmoid(gate) * value
             for kk_hi in range(3):
-                at = side * 18 + step * 6 + part * 3 + kk_hi
+                at = side * 18 + part * 3 + kk_hi
                 wide_ref[pl.ds(at, 128, stride=36), :] = out[:, kk_hi * 128 : kk_hi * 128 + 128]
-
-    @pl.when(step == 2)
-    def _():
-        out_ref[...] = wide_ref[...].astype(BF16)
+    out_ref[...] = wide_ref[...].astype(BF16)
 
 
 def project(pair, mask, gain, bias, w_proj):
     return pl.pallas_call(
         project_kernel,
-        grid=(3,),
-        out_shape=jax.ShapeDtypeStruct((4608, 128), BF16),
-        in_specs=[
-            pl.BlockSpec((16, 48, 128), lambda i: (i, 0, 0)),
-            pl.BlockSpec((16, 48), lambda i: (i, 0)),
-            full(1, 128),
-            full(1, 128),
-            full(128, 512),
+        out_shape=pltpu.VMEM((4608, 128), BF16),
+        in_specs=[pl.BlockSpec(memory_space=pltpu.HBM)] * 5,
+        out_specs=pl.BlockSpec(memory_space=pltpu.VMEM),
+        scratch_shapes=[
+            pltpu.VMEM((48, 48, 128), F32),
+            pltpu.VMEM((48, 48), jnp.int32),
+            pltpu.VMEM((1, 128), F32),
+            pltpu.VMEM((1, 128), F32),
+            pltpu.VMEM((128, 512), BF16),
+            pltpu.VMEM((512, 128), BF16),
+            pltpu.VMEM((4608, 128), F32),
+            pltpu.SemaphoreType.DMA((10,)),
         ],
-        out_specs=full(4608, 128),
-        scratch_shapes=[pltpu.VMEM((512, 128), BF16), pltpu.VMEM((4608, 128), F32)],
-        compiler_params=pltpu.CompilerParams(vmem_limit_bytes=60 << 20),
+        compiler_params=pltpu.CompilerParams(vmem_limit_bytes=32 << 20),
         name="project",
-    )(pair, mask, gain, bias, w_proj)
+    )(*(pltpu.with_memory_space_constraint(x, pltpu.HBM) for x in (pair, mask, gain, bias, w_proj)))
 
 
 def gather_kernel(core_ref, recv_ref, swap_ref, send_ref, keep_ref, wide_ref, x_ref, right_ref):
@@ -177,38 +187,31 @@
     )(pair, gain, bias, w_gate)
 
 
-def finish_kernel(mixed_ref, gate_ref, gain_ref, bias_ref, w_ref, out_ref, wide_ref):
-    step = pl.program_id(0)
-
-    @pl.when(step == 0)
-    def _():
-        wide_ref[...] = mixed_ref[...].astype(F32)
-
+def finish_kernel(mixed_ref, gate_ref, gain_ref, bias_ref, w_ref, out_hbm, wide_ref, out_ref, sems):
+    wide_ref[...] = mixed_ref[...].astype(F32)
     gain, bias = column(gain_ref[...]), column(bias_ref[...])
-    for part in range(2):
-        at = step * 6 + part * 3
+    copies = []
+    for part in range(6):
         for jj_hi in range(3):
-            mixed = wide_ref[pl.ds(at + jj_hi, 128, stride=18), :]
+            mixed = wide_ref[pl.ds(part * 3 + jj_hi, 128, stride=18), :]
             normed = layer_norm(mixed, gain, bias, 0).astype(BF16)
             projected = lax.dot_general(normed, w_ref[...], TN, preferred_element_type=F32).reshape(8, 16, 128)
             rows, cols = slice(part * 8, part * 8 + 8), slice(jj_hi * 16, jj_hi * 16 + 16)
             out_ref[rows, cols, :] = gate_ref[rows, cols, :] * projected
+        rows = pl.ds(part * 8, 8)
+        copies.append(pltpu.make_async_copy(out_ref.at[rows], out_hbm.at[rows], sems.at[part]))
+        copies[-1].start()
+    for copy in copies:
+        copy.wait()
 
 
 def finish(mixed, gate, gain, bias, w_out):
     return pl.pallas_call(
         finish_kernel,
-        grid=(3,),
         out_shape=jax.ShapeDtypeStruct((48, 48, 128), F32),
-        in_specs=[
-            full(2304, 128),
-            pl.BlockSpec((16, 48, 128), lambda i: (i, 0, 0)),
-            full(1, 128),
-            full(1, 128),
-            full(128, 128),
-        ],
-        out_specs=pl.BlockSpec((16, 48, 128), lambda i: (i, 0, 0)),
-        scratch_shapes=[pltpu.VMEM((2304, 128), F32)],
+        in_specs=[pl.BlockSpec(memory_space=pltpu.VMEM)] * 5,
+        out_specs=pl.BlockSpec(memory_space=pltpu.HBM),
+        scratch_shapes=[pltpu.VMEM((2304, 128), F32), pltpu.VMEM((48, 48, 128), F32), pltpu.SemaphoreType.DMA((6,))],
         compiler_params=pltpu.CompilerParams(vmem_limit_bytes=32 << 20),
         name="finish",
     )(mixed, gate, gain, bias, w_out)
@@ -221,15 +224,21 @@
 
 
 def per_device(pair, pair_mask, ln_gain, ln_bias, w_proj, w_gate, out_gain, out_bias, w_out):
-    recv = exchange(project(pair, pair_mask, ln_gain.reshape(1, 128), ln_bias.reshape(1, 128), w_proj))
-    gate = gating(pair, ln_gain.reshape(1, 128), ln_bias.reshape(1, 128), w_gate)
-    place = jnp.arange(1024)
-    target = place // 16 % 8 * 128 + place // 128 * 16 + place % 16
-    swap = (target[:, None] == place[None, :]).astype(BF16)
+    hold = lax.optimization_barrier
+    gain, bias = ln_gain.reshape(1, 128), ln_bias.reshape(1, 128)
+    sent = project(pair, pair_mask, gain, bias, w_proj)
     core = lax.axis_index("core").astype(jnp.int32).reshape(1)
+    sent, core = hold((sent, core))
+    recv, pair, gain, bias, w_gate, w_out, out_gain, out_bias = hold(
+        (exchange(sent), pair, gain, bias, w_gate, w_out, out_gain, out_bias)
+    )
+    place = np.arange(1024)
+    swap = jnp.asarray(place[None, :] == (place // 16 % 8 * 128 + place // 128 * 16 + place % 16)[:, None], BF16)
     mine, keep = gather(core, recv, swap)
     other = lax.ppermute(mine, "core", [(0, 1), (1, 0)])
-    mixed = exchange(contract(mine, other, keep, swap))
+    gate = gating(pair, gain, bias, w_gate)
+    sent, gate, w_out, out_gain, out_bias = hold((contract(mine, other, keep, swap), gate, w_out, out_gain, out_bias))
+    mixed, gate, w_out, out_gain, out_bias = hold((exchange(sent), gate, w_out, out_gain, out_bias))
     return finish(mixed, gate, out_gain.reshape(1, 128), out_bias.reshape(1, 128), w_out)
 
 

time: 90.7 us -> 86.8 us (0.957)
  blocking collectives: 0 us -> 75.7 us
  waiting for transfers between devices: 54.3 us -> 1.08 us
  starting transfers between devices: 22.4 us -> 0.09 us
  Pallas kernels: 13.2 us -> 9.59 us
    all_to_all x0 -> x2, blocking collectives: none -> 75.7 us  [exchange(): lax.all_to_all(tiles, GROUP, 0, 0, tiled=True).reshape(128 * rows, 128)]
    all_to_all x2 -> x0, waiting for transfers between devices: 51.9 us -> none  [exchange(): lax.all_to_all(tiles, GROUP, 0, 0, tiled=True).reshape(128 * rows, 128)]
    all_to_all x2 -> x0, starting transfers between devices: 22.3 us -> none  [exchange(): lax.all_to_all(tiles, GROUP, 0, 0, tiled=True).reshape(128 * rows, 128)]
    pallas_call x2, Pallas kernels: 7.35 us -> 4.47 us  [the longest x1 2.89 us: project(): pl.pallas_call(project_kernel, out_shape=pltpu.VMEM((4608, 128), BF16), i...]
    ppermute x1, waiting for transfers between devices: 2.41 us -> 1.08 us  [per_device(): other = lax.ppermute(mine, 'core', [(0, 1), (1, 0)])]
  transfers between devices with their start and end apart: 3 -> 1, of which waited for: 3 -> 1; matrix products, arithmetic and copies ran while one was open for 0% -> 0% of each run, Pallas kernels for 1% -> 1%
where the time goes in v4:
time: 86.8 us; the launch traced here: 86.6 us
  blocking collectives  75.7 us (87%)
  Pallas kernels  9.59 us (11%)
  waiting for transfers between devices  1.08 us (1%)
    all_to_all x2, blocking collectives, exchange(): lax.all_to_all(tiles, GROUP, 0, 0, tiled=True).reshape(128 * rows, 128)  75.7 us
    pallas_call x1, Pallas kernels, project(): pl.pallas_call(project_kernel, out_shape=pltpu.VMEM((4608, 128), BF16), i...  2.89 us
    pallas_call x1, Pallas kernels, contract(): pl.pallas_call(contract_kernel, out_shape=jax.ShapeDtypeStruct((2304, 128...  1.98 us
    pallas_call x1, Pallas kernels, gather(): pl.pallas_call(gather_kernel, out_shape=(jax.ShapeDtypeStruct((1152, 384)...  1.86 us
  transfers between devices with their start and end apart: 1, of which 1 were waited for; matrix products, arithmetic and copies ran while one was open for 0% of the time, Pallas kernels for 1%

profile of v4, /device:TPU:32, one launch (start us, length us, event | category | flops | bytes accessed | tf_op | source)
XLA Modules:
  0.0 86.6 jit_solution(12699150947826921121)
XLA Ops:
  0.0 2.9 %project.1 = bf16[4608,128]{1,0:T(8,128)(2,1)S(1)} custom-call(f32[48,48,128]{2,1,0:T(8,128)} %pair_ref, s32[48,48]{1,0:T(8,128)} %mask_hbm.1, f32[1,128]{1,0:T(1,128)} %bitcast.13, f32[1,128]{1,0:T(1,128)} %bitcast.15, bf16[128,512]{1,0:T(8,128)(2,1)} %w_hbm.1), custom_call_target="tpu_custom_call" | custom-call | tf_op jit(solution)/shard_map/project/pallas_call | solution.py:81
  2.9 0.0 copy-start
  2.9 47.8 %all_to_all.10 = bf16[128,9,4,128]{3,2,1,0:T(4,128)(2,1)S(1)} all-to-all(bf16[128,9,4,128]{3,2,1,0:T(4,128)(2,1)S(1)} %bitcast.10), channel_id=1, replica_groups=mesh['xh'=2,'zh'=4,'zl'=2,'xl'=2,'y'=4,'core'=2] {'y','zh','zl','xh','xl'}, dimensions={0} | all-to-all | bytes 2359296 | tf_op jit(solution)/shard_map/all_to_all | solution.py:223
  50.7 0.0 copy-done
  50.7 0.0 copy-start.1
  50.7 0.0 copy-start.2
  50.7 0.0 copy-start.4
  50.7 0.0 copy-start.5
  50.7 1.9 %gather.1 = (bf16[1152,384]{1,0:T(8,128)(2,1)S(1)}, bf16[384,384]{1,0:T(8,128)(2,1)S(1)}) custom-call(s32[1]{0:T(128)} %bitcast.2.core_ref, bf16[4608,128]{1,0:T(8,128)(2,1)S(1)} %bitcast.9, bf16[1024,1024]{1,0:T(8,128)(2,1)S(1)} %copy-done), custom_call_target="tpu_custom_call" | custom-call | tf_op jit(solution)/shard_map/gather/pallas_call | solution.py:131
  52.6 0.1 collective-permute-start
  52.7 0.0 copy-done.1
  52.7 0.0 copy-done.2
  52.7 0.0 copy-done.4
  52.7 0.0 copy-done.5
  52.7 1.3 %gate.1.gate_ref = f32[48,48,128]{2,1,0:T(8,128)S(1)} custom-call(f32[48,48,128]{2,1,0:T(8,128)S(1)} %copy-done.1, f32[1,128]{1,0:T(1,128)S(1)} %bitcast.14, f32[1,128]{1,0:T(1,128)S(1)} %bitcast.16, bf16[128,128]{1,0:T(8,128)(2,1)S(1)} %copy-done.2), custom_call_target="tpu_custom_call" | custom-call | flops 75000000 | bytes 2400000 | tf_op jit(solution)/shard_map/gate/pallas_call | solution.py:178
  54.0 1.1 %collective-permute-done.other_ref = bf16[1152,384]{1,0:T(8,128)(2,1)S(1)} collective-permute-done((bf16[1152,384]{1,0:T(8,128)(2,1)S(1)}, bf16[1152,384]{1,0:T(8,128)(2,1)S(1)}, u32[]{:S(2)}, u32[]{:S(2)}) %collective-permute-start) | collective-permute-done | bytes 884768 | tf_op jit(solution)/shard_map/ppermute | solution.py:238
  55.1 2.0 %contract.1 = bf16[2304,128]{1,0:T(8,128)(2,1)S(1)} custom-call(bf16[1152,384]{1,0:T(8,128)(2,1)S(1)} %get-tuple-element.30.mine_ref, bf16[1152,384]{1,0:T(8,128)(2,1)S(1)} %collective-permute-done.other_ref, bf16[384,384]{1,0:T(8,128)(2,1)S(1)} %get-tuple-element.31.keep_ref, bf16[1024,1024]{1,0:T(8,128)(2,1)S(1)} %copy-done), custom_call_target="tpu_custom_call" | custom-call | tf_op jit(solution)/shard_map/contract/pallas_call | solution.py:161
  57.1 0.0 copy-start.3
  57.1 0.0 copy-start.6
  57.1 0.0 copy-start.7
  57.1 27.9 %all_to_all.11 = bf16[128,9,2,128]{3,2,1,0:T(2,128)(2,1)S(1)} all-to-all(bf16[128,9,2,128]{3,2,1,0:T(2,128)(2,1)S(1)} %bitcast.11), channel_id=1, replica_groups=mesh['xh'=2,'zh'=4,'zl'=2,'xl'=2,'y'=4,'core'=2] {'y','zh','zl','xh','xl'}, dimensions={0} | all-to-all | bytes 1179648 | tf_op jit(solution)/shard_map/all_to_all | solution.py:223
  85.0 0.0 copy-done.3
  85.0 0.0 copy-done.6
  85.0 0.0 copy-done.7
  85.0 1.6 %finish.1 = f32[48,48,128]{2,1,0:T(8,128)} custom-call(bf16[2304,128]{1,0:T(8,128)(2,1)S(1)} %bitcast.12, f32[48,48,128]{2,1,0:T(8,128)S(1)} %gate.1.gate_ref, f32[1,128]{1,0:T(1,128)S(1)} %bitcast.17, f32[1,128]{1,0:T(1,128)S(1)} %bitcast.18, bf16[128,128]{1,0:T(8,128)(2,1)S(1)} %copy-done.3), custom_call_target="tpu_custom_call" | custom-call | tf_op jit(solution)/shard_map/finish/pallas_call | solution.py:209
Async XLA Ops:
  2.9 47.8 %copy-start = (bf16[1024,1024]{1,0:T(8,128)(2,1)S(1)}, bf16[1024,1024]{1,0:T(8,128)(2,1)}, u32[]{:S(2)}) copy-start(bf16[1024,1024]{1,0:T(8,128)(2,1)} %constant.6.clone.swap_ref) | copy-start | bytes 6291460
  50.7 2.0 %copy-start.1 = (f32[48,48,128]{2,1,0:T(8,128)S(1)}, f32[48,48,128]{2,1,0:T(8,128)}, u32[]{:S(2)}) copy-start(f32[48,48,128]{2,1,0:T(8,128)} %pair_ref) | copy-start | bytes 3538948
  50.7 2.0 %copy-start.2 = (bf16[128,128]{1,0:T(8,128)(2,1)S(1)}, bf16[128,128]{1,0:T(8,128)(2,1)}, u32[]{:S(2)}) copy-start(bf16[128,128]{1,0:T(8,128)(2,1)} %w_ref) | copy-start | bytes 98308
  50.7 2.0 %copy-start.4 = (f32[128]{0:T(128)S(1)}, f32[128]{0:T(128)}, u32[]{:S(2)}) copy-start(f32[128]{0:T(128)} %param.12) | copy-start | bytes 1540
  50.7 2.0 %copy-start.5 = (f32[128]{0:T(128)S(1)}, f32[128]{0:T(128)}, u32[]{:S(2)}) copy-start(f32[128]{0:T(128)} %param.13) | copy-start | bytes 1540
  52.6 2.5 %collective-permute-start = (bf16[1152,384]{1,0:T(8,128)(2,1)S(1)}, bf16[1152,384]{1,0:T(8,128)(2,1)S(1)}, u32[]{:S(2)}, u32[]{:S(2)}) collective-permute-start(bf16[1152,384]{1,0:T(8,128)(2,1)S(1)} %get-tuple-element.30.mine_ref), channel_id=1, source_target_pairs={{0,1},{1,0},{2,3},{3,2},{4,5},{5,4},{6,7},{7,6},{8,9},{9,8},{10,11... | collective-permute-start | bytes 2654216 | tf_op jit(solution)/shard_map/ppermute | solution.py:238
  57.1 28.0 %copy-start.3 = (bf16[128,128]{1,0:T(8,128)(2,1)S(1)}, bf16[128,128]{1,0:T(8,128)(2,1)}, u32[]{:S(2)}) copy-start(bf16[128,128]{1,0:T(8,128)(2,1)} %w_ref.1) | copy-start | bytes 98308
  57.1 27.9 %copy-start.6 = (f32[128]{0:T(128)S(1)}, f32[128]{0:T(128)}, u32[]{:S(2)}) copy-start(f32[128]{0:T(128)} %param.16) | copy-start | bytes 1540
  57.1 27.9 %copy-start.7 = (f32[128]{0:T(128)S(1)}, f32[128]{0:T(128)}, u32[]{:S(2)}) copy-start(f32[128]{0:T(128)} %param.17) | copy-start | bytes 1540

commit v5 on v4

v5 whole, which is shorter than its diff:
```python
import jax
import jax.numpy as jnp
import numpy as np
from jax import lax
from jax.experimental import pallas as pl
from jax.experimental.pallas import tpu as pltpu
from jax.sharding import Mesh, PartitionSpec as P

EPS = 1e-05
ROW = ("xh", "zh", "zl")
COL = ("xl", "y", "core")
GROUP = ("y", "zh", "zl", "xh", "xl")
F32, BF16 = jnp.float32, jnp.bfloat16
NT = (((1,), (1,)), ((), ()))
TN = (((0,), (0,)), ((), ()))


def sigmoid(x):
    return 0.5 * jnp.tanh(0.5 * x) + 0.5


def layer_norm(x, gain, bias, axis):
    mean = jnp.mean(x, axis=axis, keepdims=True)
    centred = x - mean
    var = jnp.mean(centred * centred, axis=axis, keepdims=True)
    return centred * lax.rsqrt(var + EPS) * gain + bias


def column(row):
    return jnp.broadcast_to(row, (8, 128)).T[:, :1]


def full(*shape):
    return pl.BlockSpec(shape, lambda i: (0,) * len(shape))


def rows_of(place, pair, rows):
    return pl.ds((pair // 2 * 32 + pair % 2) * rows + place, 16, stride=2 * rows)


def project_kernel(
    pair_hbm, mask_hbm, gain_hbm, bias_hbm, w_hbm, w_gate_hbm, out_ref, gate_ref,
    pair_ref, mask_ref, gain_ref, bias_ref, w_ref, w_gate_ref, wt_ref, normed_ref, wide_ref, sems,
):
    small = [
        pltpu.make_async_copy(src, dst, sems.at[6 + n])
        for n, (src, dst) in enumerate(
            (
                (w_hbm, w_ref),
                (gain_hbm, gain_ref),
                (bias_hbm, bias_ref),
                (mask_hbm, mask_ref),
                (w_gate_hbm, w_gate_ref),
            )
        )
    ]
    chunks = [
        pltpu.make_async_copy(pair_hbm.at[pl.ds(part * 8, 8)], pair_ref.at[pl.ds(part * 8, 8)], sems.at[part])
        for part in range(6)
    ]
    for copy in chunks[:2] + small + chunks[2:]:
        copy.start()
    lane = lax.broadcasted_iota(jnp.int32, (48, 384), 1)
    row = lax.broadcasted_iota(jnp.int32, (48, 384), 0)
    spread = (lane // 128 * 16 + lane % 16 == row).astype(F32).astype(BF16)
    own = lax.broadcasted_iota(jnp.int32, (8, 384), 1) // 16 % 8 == lax.broadcasted_iota(jnp.int32, (8, 384), 0)
    for copy in small + chunks[:2]:
        copy.wait()
    wt_ref[...] = w_ref[...].astype(F32).T.astype(BF16)
    keeps = jnp.dot(mask_ref[...].astype(F32).astype(BF16), spread, preferred_element_type=F32)
    gain, bias = column(gain_ref[...]), column(bias_ref[...])

    def norm(part):
        x = pair_ref[part * 8 : part * 8 + 8].reshape(8, 3, 16, 128).transpose(1, 0, 2, 3).reshape(384, 128)
        return layer_norm(x.T, gain, bias, 0).astype(BF16)

    for part in range(2):
        normed_ref[part] = norm(part)
    for copy in chunks[2:]:
        copy.wait()
    for part in range(6):
        normed = normed_ref[part] if part < 2 else norm(part)
        keep = jnp.sum(jnp.where(own, keeps[part * 8 : part * 8 + 8], 0.0), axis=0, keepdims=True)
        for side in range(2):
            gate = jnp.dot(wt_ref[side * 256 : side * 256 + 128, :], normed, preferred_element_type=F32)
            value = jnp.dot(wt_ref[side * 256 + 128 : side * 256 + 256, :], normed, preferred_element_type=F32)
            out = keep * sigmoid(gate) * value
            for kk_hi in range(3):
                at = side * 18 + part * 3 + kk_hi
                wide_ref[pl.ds(at, 128, stride=36), :] = out[:, kk_hi * 128 : kk_hi * 128 + 128]
        gate = sigmoid(lax.dot_general(normed, w_gate_ref[...], TN, preferred_element_type=F32))
        gate_ref[part * 8 : part * 8 + 8] = gate.reshape(3, 8, 16, 128).transpose(1, 0, 2, 3).reshape(8, 48, 128)
    out_ref[...] = wide_ref[...].astype(BF16)


def project(pair, mask, gain, bias, w_proj, w_gate):
    return pl.pallas_call(
        project_kernel,
        out_shape=(pltpu.VMEM((4608, 128), BF16), pltpu.VMEM((48, 48, 128), F32)),
        in_specs=[pl.BlockSpec(memory_space=pltpu.HBM)] * 6,
        out_specs=(pl.BlockSpec(memory_space=pltpu.VMEM), pl.BlockSpec(memory_space=pltpu.VMEM)),
        scratch_shapes=[
            pltpu.VMEM((48, 48, 128), F32),
            pltpu.VMEM((48, 48), jnp.int32),
            pltpu.VMEM((1, 128), F32),
            pltpu.VMEM((1, 128), F32),
            pltpu.VMEM((128, 512), BF16),
            pltpu.VMEM((128, 128), BF16),
            pltpu.VMEM((512, 128), BF16),
            pltpu.VMEM((6, 128, 384), BF16),
            pltpu.VMEM((4608, 128), F32),
            pltpu.SemaphoreType.DMA((11,)),
        ],
        compiler_params=pltpu.CompilerParams(vmem_limit_bytes=32 << 20),
        name="project",
    )(*(pltpu.with_memory_space_constraint(x, pltpu.HBM) for x in (pair, mask, gain, bias, w_proj, w_gate)))


def unmix(recv_ref, swap_ref, wide_ref, x_ref, dst_ref, side):
    wide_ref[...] = recv_ref[...].astype(F32)
    for s in range(18):
        for c in range(8):
            rows = wide_ref[rows_of(side * 18 + s, c, 36), :]
            x_ref[s * 16 : s * 16 + 16, c * 128 : c * 128 + 128] = rows.astype(BF16)
    for n in range(4):
        y = jnp.dot(x_ref[...], swap_ref[:, n * 256 : n * 256 + 256], preferred_element_type=F32).astype(BF16)
        for half in range(2):
            for s in range(18):
                at = (s // 3 * 8 + 2 * n + half) * 16
                lanes = slice(s % 3 * 128, s % 3 * 128 + 128)
                dst_ref[at : at + 16, lanes] = y[s * 16 : s * 16 + 16, half * 128 : half * 128 + 128]


def gather_left_kernel(recv_ref, swap_ref, out_ref, wide_ref, x_ref):
    unmix(recv_ref, swap_ref, wide_ref, x_ref, out_ref, 0)


def gather_right_kernel(core_ref, recv_ref, swap_ref, send_ref, keep_ref, wide_ref, x_ref, right_ref):
    unmix(recv_ref, swap_ref, wide_ref, x_ref, right_ref, 1)
    row = lax.broadcasted_iota(jnp.int32, (128, 256), 0)
    lane = lax.broadcasted_iota(jnp.int32, (128, 256), 1)
    b = row // 16
    for dst_ref, core in ((keep_ref, core_ref[0]), (send_ref, 1 - core_ref[0])):
        pick = (lane // 16 == row % 16) & (lane % 16 == b // 2 * 4 + core * 2 + b % 2)
        pick = pick.astype(F32).astype(BF16)
        for jj_hi in range(3):
            rows = jnp.dot(pick, right_ref[jj_hi * 256 : jj_hi * 256 + 256, :], preferred_element_type=F32)
            dst_ref[jj_hi * 128 : jj_hi * 128 + 128, :] = rows.astype(BF16)


UNMIX_SCRATCH = [pltpu.VMEM((4608, 128), F32), pltpu.VMEM((288, 1024), BF16)]


def gather_left(recv, swap):
    return pl.pallas_call(
        gather_left_kernel,
        out_shape=jax.ShapeDtypeStruct((768, 384), BF16),
        scratch_shapes=UNMIX_SCRATCH,
        compiler_params=pltpu.CompilerParams(vmem_limit_bytes=32 << 20),
        name="gather_left",
    )(recv, swap)


def gather_right(core, recv, swap):
    vmem = pl.BlockSpec(memory_space=pltpu.VMEM)
    half = jax.ShapeDtypeStruct((384, 384), BF16)
    return pl.pallas_call(
        gather_right_kernel,
        out_shape=(half, half),
        in_specs=[pl.BlockSpec(memory_space=pltpu.SMEM), vmem, vmem],
        out_specs=(vmem, vmem),
        scratch_shapes=UNMIX_SCRATCH + [pltpu.VMEM((768, 384), BF16)],
        compiler_params=pltpu.CompilerParams(vmem_limit_bytes=32 << 20),
        name="gather_right",
    )(core, recv, swap)


def contract_own_kernel(left_ref, right_ref, out_ref):
    for i in range(6):
        rows = slice(i * 128, i * 128 + 128)
        out_ref[rows, :] = lax.dot_general(left_ref[rows, :], right_ref[...], NT, preferred_element_type=F32)


def contract_own(left, right):
    return pl.pallas_call(
        contract_own_kernel,
        out_shape=jax.ShapeDtypeStruct((768, 384), F32),
        compiler_params=pltpu.CompilerParams(vmem_limit_bytes=32 << 20),
        cost_estimate=pl.CostEstimate(flops=2 * 768 * 384 * 384, bytes_accessed=2_000_000, transcendentals=0),
        name="contract_own",
    )(left, right)


def contract_kernel(own_ref, left_ref, right_ref, swap_ref, out_ref, x_ref, wide_ref):
    for i in range(6):
        rows = slice(i * 128, i * 128 + 128)
        mixed = lax.dot_general(left_ref[rows, :], right_ref[...], NT, preferred_element_type=F32)
        mixed = (own_ref[rows, :] + mixed).astype(BF16)
        for j in range(3):
            for a in range(8):
                at = (i * 3 + j) * 16
                x_ref[at : at + 16, a * 128 : a * 128 + 128] = mixed[a * 16 : a * 16 + 16, j * 128 : j * 128 + 128]
    for n in range(4):
        y = jnp.dot(x_ref[...], swap_ref[:, n * 256 : n * 256 + 256], preferred_element_type=F32)
        for half in range(2):
            for s in range(18):
                wide_ref[rows_of(s, 2 * n + half, 18), :] = y[s * 16 : s * 16 + 16, half * 128 : half * 128 + 128]
    out_ref[...] = wide_ref[...].astype(BF16)


def contract(own, left, right, swap):
    return pl.pallas_call(
        contract_kernel,
        out_shape=jax.ShapeDtypeStruct((2304, 128), BF16),
        scratch_shapes=[pltpu.VMEM((288, 1024), BF16), pltpu.VMEM((2304, 128), F32)],
        compiler_params=pltpu.CompilerParams(vmem_limit_bytes=32 << 20),
        name="contract",
    )(own, left, right, swap)


def finish_kernel(mixed_ref, gate_ref, gain_ref, bias_ref, w_ref, out_hbm, wide_ref, out_ref, sems):
    wide_ref[...] = mixed_ref[...].astype(F32)
    gain, bias = column(gain_ref[...]), column(bias_ref[...])
    copies = []
    for part in range(6):
        for jj_hi in range(3):
            mixed = wide_ref[pl.ds(part * 3 + jj_hi, 128, stride=18), :]
            normed = layer_norm(mixed, gain, bias, 0).astype(BF16)
            projected = lax.dot_general(normed, w_ref[...], TN, preferred_element_type=F32).reshape(8, 16, 128)
            rows, cols = slice(part * 8, part * 8 + 8), slice(jj_hi * 16, jj_hi * 16 + 16)
            out_ref[rows, cols, :] = gate_ref[rows, cols, :] * projected
        rows = pl.ds(part * 8, 8)
        copies.append(pltpu.make_async_copy(out_ref.at[rows], out_hbm.at[rows], sems.at[part]))
        copies[-1].start()
    for copy in copies:
        copy.wait()


def finish(mixed, gate, gain, bias, w_out):
    return pl.pallas_call(
        finish_kernel,
        out_shape=jax.ShapeDtypeStruct((48, 48, 128), F32),
        in_specs=[pl.BlockSpec(memory_space=pltpu.VMEM)] * 5,
        out_specs=pl.BlockSpec(memory_space=pltpu.HBM),
        scratch_shapes=[pltpu.VMEM((2304, 128), F32), pltpu.VMEM((48, 48, 128), F32), pltpu.SemaphoreType.DMA((6,))],
        compiler_params=pltpu.CompilerParams(vmem_limit_bytes=32 << 20),
        name="finish",
    )(mixed, gate, gain, bias, w_out)


def exchange(messages):
    rows = messages.shape[0] // 128
    tiles = messages.reshape(128, 9, rows // 9, 128)
    return lax.all_to_all(tiles, GROUP, 0, 0, tiled=True).reshape(128 * rows, 128)


def per_device(pair, pair_mask, ln_gain, ln_bias, w_proj, w_gate, out_gain, out_bias, w_out):
    hold = lax.optimization_barrier
    sent, gate = project(pair, pair_mask, ln_gain.reshape(1, 128), ln_bias.reshape(1, 128), w_proj, w_gate)
    core = lax.axis_index("core").astype(jnp.int32).reshape(1)
    sent, gate, core = hold((sent, gate, core))
    recv, gate, w_out, out_gain, out_bias = hold((exchange(sent), gate, w_out, out_gain, out_bias))
    place = np.arange(1024)
    swap = jnp.asarray(place[None, :] == (place // 16 % 8 * 128 + place // 128 * 16 + place % 16)[:, None], BF16)
    swap_cores = lambda v: lax.ppermute(v, "core", [(0, 1), (1, 0)])
    left = gather_left(recv, swap)
    left2 = swap_cores(left)
    right_send, right = gather_right(core, recv, swap)
    right2 = swap_cores(right_send)
    own = contract_own(left, right)
    sent = contract(own, left2, right2, swap)
    sent, gate, w_out, out_gain, out_bias = hold((sent, gate, w_out, out_gain, out_bias))
    mixed, gate, w_out, out_gain, out_bias = hold((exchange(sent), gate, w_out, out_gain, out_bias))
    return finish(mixed, gate, out_gain.reshape(1, 128), out_bias.reshape(1, 128), w_out)


def solution(mesh):
    fine = Mesh(mesh.devices.reshape(2, 4, 2, 2, 4, 2), ROW + COL)
    return jax.shard_map(
        per_device,
        mesh=fine,
        in_specs=(P(ROW, COL, None), P(ROW, COL), P(), P(), P(), P(), P(), P(), P()),
        out_specs=P(ROW, COL, None),
        check_vma=False,
    )
```

time: 86.8 us -> 86 us (level)
  Pallas kernels: 9.59 us -> 8.63 us
    pallas_call x3 -> x4, Pallas kernels: 6.03 us -> 5.7 us  [the longest x1 2.84 us: project(): pl.pallas_call(project_kernel, out_shape=(pltpu.VMEM((4608, 128), BF16),...]
  transfers between devices with their start and end apart: 1 -> 2, of which waited for: 1 -> 1; matrix products, arithmetic and copies ran while one was open for 0% -> 0% of each run, Pallas kernels for 1% -> 2%
where the time goes in v5:
time: 86 us; the launch traced here: 85.8 us
  blocking collectives  75.9 us (88%)
  Pallas kernels  8.63 us (10%)
    all_to_all x2, blocking collectives, exchange(): lax.all_to_all(tiles, GROUP, 0, 0, tiled=True).reshape(128 * rows, 128)  75.9 us
    pallas_call x1, Pallas kernels, project(): pl.pallas_call(project_kernel, out_shape=(pltpu.VMEM((4608, 128), BF16),...  2.84 us
  transfers between devices with their start and end apart: 2, of which 1 were waited for; matrix products, arithmetic and copies ran while one was open for 0% of the time, Pallas kernels for 2%

profile of v5, /device:TPU:32, one launch (start us, length us, event | category | flops | bytes accessed | tf_op | source)
XLA Modules:
  0.0 85.8 jit_solution(3458636501051750721)
XLA Ops:
  0.0 2.8 %project.1 = (bf16[4608,128]{1,0:T(8,128)(2,1)S(1)}, f32[48,48,128]{2,1,0:T(8,128)S(1)}) custom-call(f32[48,48,128]{2,1,0:T(8,128)} %pair_hbm.1, s32[48,48]{1,0:T(8,128)} %mask_hbm.1, f32[1,128]{1,0:T(1,128)} %bitcast.16, f32[1,128]{1,0:T(1,128)} %bitcast.17, bf16[128,512]{1,0:T(8,128)(2,1)} %w_hbm.1, bf16[128,128]{1,0:T(8,128)(2,1)} %w_gate_hbm.1), custom_call_target="tpu_custom_call" | custom-call | tf_op jit(solution)/shard_map/project/pallas_call | solution.py:97
  2.9 0.0 copy-start
  2.9 47.8 %all_to_all.10 = bf16[128,9,4,128]{3,2,1,0:T(4,128)(2,1)S(1)} all-to-all(bf16[128,9,4,128]{3,2,1,0:T(4,128)(2,1)S(1)} %bitcast.13), channel_id=1, replica_groups=mesh['xh'=2,'zh'=4,'zl'=2,'xl'=2,'y'=4,'core'=2] {'y','zh','zl','xh','xl'}, dimensions={0} | all-to-all | bytes 2359296 | tf_op jit(solution)/shard_map/all_to_all | solution.py:254
  50.6 0.0 copy-done
  50.6 0.9 %gather_left.1.left_ref = bf16[768,384]{1,0:T(8,128)(2,1)S(1)} custom-call(bf16[4608,128]{1,0:T(8,128)(2,1)S(1)} %bitcast.9, bf16[1024,1024]{1,0:T(8,128)(2,1)S(1)} %copy-done), custom_call_target="tpu_custom_call" | custom-call | tf_op jit(solution)/shard_map/gather_left/pallas_call | solution.py:155
  51.6 0.1 collective-permute-start
  51.7 1.3 %gather_right.1 = (bf16[384,384]{1,0:T(8,128)(2,1)S(1)}, bf16[384,384]{1,0:T(8,128)(2,1)S(1)}) custom-call(s32[1]{0:T(128)} %bitcast.2.core_ref, bf16[4608,128]{1,0:T(8,128)(2,1)S(1)} %bitcast.10, bf16[1024,1024]{1,0:T(8,128)(2,1)S(1)} %copy-done), custom_call_target="tpu_custom_call" | custom-call | tf_op jit(solution)/shard_map/gather_right/pallas_call | solution.py:167
  52.9 0.6 collective-permute-start.1
  53.5 0.7 contract_own.1.own_ref
  54.2 0.5 collective-permute-done.1.right_ref
  54.7 0.0 collective-permute-done.left_ref
  54.7 1.4 %contract.1 = bf16[2304,128]{1,0:T(8,128)(2,1)S(1)} custom-call(f32[768,384]{1,0:T(8,128)S(1)} %contract_own.1.own_ref, bf16[768,384]{1,0:T(8,128)(2,1)S(1)} %collective-permute-done.left_ref, bf16[384,384]{1,0:T(8,128)(2,1)S(1)} %collective-permute-done.1.right_ref, bf16[1024,1024]{1,0:T(8,128)(2,1)S(1)} %copy-done), custom_call_target="tpu_custom_call" | custom-call | tf_op jit(solution)/shard_map/contract/pallas_call | solution.py:212
  56.1 0.0 copy-start.1
  56.1 0.0 copy-start.2
  56.1 0.0 copy-start.3
  56.1 28.1 %all_to_all.11 = bf16[128,9,2,128]{3,2,1,0:T(2,128)(2,1)S(1)} all-to-all(bf16[128,9,2,128]{3,2,1,0:T(2,128)(2,1)S(1)} %bitcast.11), channel_id=1, replica_groups=mesh['xh'=2,'zh'=4,'zl'=2,'xl'=2,'y'=4,'core'=2] {'y','zh','zl','xh','xl'}, dimensions={0} | all-to-all | bytes 1179648 | tf_op jit(solution)/shard_map/all_to_all | solution.py:254
  84.2 0.0 copy-done.1
  84.2 0.0 copy-done.2
  84.2 0.0 copy-done.3
  84.2 1.6 %finish.1 = f32[48,48,128]{2,1,0:T(8,128)} custom-call(bf16[2304,128]{1,0:T(8,128)(2,1)S(1)} %bitcast.12, f32[48,48,128]{2,1,0:T(8,128)S(1)} %get-tuple-element.45.gate_ref, f32[1,128]{1,0:T(1,128)S(1)} %bitcast.14, f32[1,128]{1,0:T(1,128)S(1)} %bitcast.15, bf16[128,128]{1,0:T(8,128)(2,1)S(1)} %copy-done.1), custom_call_target="tpu_custom_call" | custom-call | tf_op jit(solution)/shard_map/finish/pallas_call | solution.py:240
Async XLA Ops:
  2.9 47.8 %copy-start = (bf16[1024,1024]{1,0:T(8,128)(2,1)S(1)}, bf16[1024,1024]{1,0:T(8,128)(2,1)}, u32[]{:S(2)}) copy-start(bf16[1024,1024]{1,0:T(8,128)(2,1)} %constant.6.clone.swap_ref) | copy-start | bytes 6291460
  51.6 3.2 %collective-permute-start = (bf16[768,384]{1,0:T(8,128)(2,1)S(1)}, bf16[768,384]{1,0:T(8,128)(2,1)S(1)}, u32[]{:S(2)}, u32[]{:S(2)}) collective-permute-start(bf16[768,384]{1,0:T(8,128)(2,1)S(1)} %gather_left.1.left_ref), channel_id=1, source_target_pairs={{0,1},{1,0},{2,3},{3,2},{4,5},{5,4},{6,7},{7,6},{8,9},{9,8},{10,11... | collective-permute-start | bytes 1769480 | tf_op jit(solution)/shard_map/ppermute | solution.py:265
  52.9 1.8 %collective-permute-start.1 = (bf16[384,384]{1,0:T(8,128)(2,1)S(1)}, bf16[384,384]{1,0:T(8,128)(2,1)S(1)}, u32[]{:S(2)}, u32[]{:S(2)}) collective-permute-start(bf16[384,384]{1,0:T(8,128)(2,1)S(1)} %get-tuple-element.34), channel_id=1, source_target_pairs={{0,1},{1,0},{2,3},{3,2},{4,5},{5,4},{6,7},{7,6},{8,9},{9,8},{10,11... | collective-permute-start | bytes 884744 | tf_op jit(solution)/shard_map/ppermute | solution.py:265
  56.1 28.2 %copy-start.1 = (bf16[128,128]{1,0:T(8,128)(2,1)S(1)}, bf16[128,128]{1,0:T(8,128)(2,1)}, u32[]{:S(2)}) copy-start(bf16[128,128]{1,0:T(8,128)(2,1)} %w_ref) | copy-start | bytes 98308
  56.1 28.1 %copy-start.2 = (f32[128]{0:T(128)S(1)}, f32[128]{0:T(128)}, u32[]{:S(2)}) copy-start(f32[128]{0:T(128)} %param.16) | copy-start | bytes 1540
  56.1 28.1 %copy-start.3 = (f32[128]{0:T(128)S(1)}, f32[128]{0:T(128)}, u32[]{:S(2)}) copy-start(f32[128]{0:T(128)} %param.17) | copy-start | bytes 1540

commit v6 on v5

--- a/solution.py
+++ b/solution.py
@@ -1,3 +1,5 @@
+import math
+
 import jax
 import jax.numpy as jnp
 import numpy as np
@@ -9,7 +11,12 @@
 EPS = 1e-05
 ROW = ("xh", "zh", "zl")
 COL = ("xl", "y", "core")
-GROUP = ("y", "zh", "zl", "xh", "xl")
+GROUP = ('zl', 'y', 'zh', 'xh', 'xl')
+SIZES = dict(zh=4, zl=2, xl=2, y=4, xh=2)
+STEP = {axis: math.prod(SIZES[later] for later in GROUP[n + 1 :]) for n, axis in enumerate(GROUP)}
+XH_FIRST = GROUP.index("xh") < GROUP.index("zh")
+B_STEP = STEP["zh" if XH_FIRST else "xh"]
+PAIR = [STEP["y"] * (c % 4 if XH_FIRST else c // 2) + STEP["xl"] * (c // 4 if XH_FIRST else c % 2) for c in range(8)]
 F32, BF16 = jnp.float32, jnp.bfloat16
 NT = (((1,), (1,)), ((), ()))
 TN = (((0,), (0,)), ((), ()))
@@ -34,8 +41,8 @@
     return pl.BlockSpec(shape, lambda i: (0,) * len(shape))
 
 
-def rows_of(place, pair, rows):
-    return pl.ds((pair // 2 * 32 + pair % 2) * rows + place, 16, stride=2 * rows)
+def rows_of(at, pair, zl, rows):
+    return pl.ds((PAIR[pair] + STEP["zl"] * zl) * rows + at, 8, stride=B_STEP * rows)
 
 
 def project_kernel(
@@ -116,63 +123,62 @@
     )(*(pltpu.with_memory_space_constraint(x, pltpu.HBM) for x in (pair, mask, gain, bias, w_proj, w_gate)))
 
 
-def unmix(recv_ref, swap_ref, wide_ref, x_ref, dst_ref, side):
+def gather_left_kernel(recv_ref, swap_ref, out_ref, wide_ref, x_ref):
     wide_ref[...] = recv_ref[...].astype(F32)
     for s in range(18):
         for c in range(8):
-            rows = wide_ref[rows_of(side * 18 + s, c, 36), :]
-            x_ref[s * 16 : s * 16 + 16, c * 128 : c * 128 + 128] = rows.astype(BF16)
+            rows = [wide_ref[rows_of(s, c, zl, 36), :] for zl in range(2)]
+            x_ref[s * 16 : s * 16 + 16, c * 128 : c * 128 + 128] = jnp.concatenate(rows).astype(BF16)
     for n in range(4):
         y = jnp.dot(x_ref[...], swap_ref[:, n * 256 : n * 256 + 256], preferred_element_type=F32).astype(BF16)
         for half in range(2):
             for s in range(18):
                 at = (s // 3 * 8 + 2 * n + half) * 16
                 lanes = slice(s % 3 * 128, s % 3 * 128 + 128)
-                dst_ref[at : at + 16, lanes] = y[s * 16 : s * 16 + 16, half * 128 : half * 128 + 128]
-
-
-def gather_left_kernel(recv_ref, swap_ref, out_ref, wide_ref, x_ref):
-    unmix(recv_ref, swap_ref, wide_ref, x_ref, out_ref, 0)
-
-
-def gather_right_kernel(core_ref, recv_ref, swap_ref, send_ref, keep_ref, wide_ref, x_ref, right_ref):
-    unmix(recv_ref, swap_ref, wide_ref, x_ref, right_ref, 1)
-    row = lax.broadcasted_iota(jnp.int32, (128, 256), 0)
-    lane = lax.broadcasted_iota(jnp.int32, (128, 256), 1)
-    b = row // 16
-    for dst_ref, core in ((keep_ref, core_ref[0]), (send_ref, 1 - core_ref[0])):
-        pick = (lane // 16 == row % 16) & (lane % 16 == b // 2 * 4 + core * 2 + b % 2)
-        pick = pick.astype(F32).astype(BF16)
+                out_ref[at : at + 16, lanes] = y[s * 16 : s * 16 + 16, half * 128 : half * 128 + 128]
+
+
+def gather_right_kernel(of_ref, recv_ref, swap_ref, out_ref, wide_ref, x_ref, rows_ref):
+    wide_ref[...] = recv_ref[...].astype(F32)
+    for s in range(0, 18, 2):
+        for c in range(8):
+            rows = [wide_ref[rows_of(18 + s + k, c, of_ref[0], 36), :] for k in range(2)]
+            x_ref[s * 8 : s * 8 + 16, c * 128 : c * 128 + 128] = jnp.concatenate(rows).astype(BF16)
+    for n in range(4):
+        y = jnp.dot(x_ref[...], swap_ref[:, n * 256 : n * 256 + 256], preferred_element_type=F32)
+        for half in range(2):
+            for s in range(18):
+                at = (s // 3 * 8 + 2 * n + half) * 8
+                rows_ref[s % 3, at : at + 8, :] = y[s * 8 : s * 8 + 8, half * 128 : half * 128 + 128]
+    for kk_hi in range(3):
         for jj_hi in range(3):
-            rows = jnp.dot(pick, right_ref[jj_hi * 256 : jj_hi * 256 + 256, :], preferred_element_type=F32)
-            dst_ref[jj_hi * 128 : jj_hi * 128 + 128, :] = rows.astype(BF16)
-
-
-UNMIX_SCRATCH = [pltpu.VMEM((4608, 128), F32), pltpu.VMEM((288, 1024), BF16)]
+            for b in range(8):
+                at = (jj_hi * 8 + b) * 16
+                rows = rows_ref[kk_hi, pl.ds(jj_hi * 128 + b, 16, stride=8), :]
+                out_ref[at : at + 16, kk_hi * 128 : kk_hi * 128 + 128] = rows.astype(BF16)
 
 
 def gather_left(recv, swap):
     return pl.pallas_call(
         gather_left_kernel,
         out_shape=jax.ShapeDtypeStruct((768, 384), BF16),
-        scratch_shapes=UNMIX_SCRATCH,
+        scratch_shapes=[pltpu.VMEM((4608, 128), F32), pltpu.VMEM((288, 1024), BF16)],
         compiler_params=pltpu.CompilerParams(vmem_limit_bytes=32 << 20),
         name="gather_left",
     )(recv, swap)
 
 
-def gather_right(core, recv, swap):
+def gather_right(of, recv, swap):
     vmem = pl.BlockSpec(memory_space=pltpu.VMEM)
-    half = jax.ShapeDtypeStruct((384, 384), BF16)
     return pl.pallas_call(
         gather_right_kernel,
-        out_shape=(half, half),
+        out_shape=jax.ShapeDtypeStruct((384, 384), BF16),
         in_specs=[pl.BlockSpec(memory_space=pltpu.SMEM), vmem, vmem],
-        out_specs=(vmem, vmem),
-        scratch_shapes=UNMIX_SCRATCH + [pltpu.VMEM((768, 384), BF16)],
+        out_specs=vmem,
+        scratch_shapes=[pltpu.VMEM((4608, 128), F32), pltpu.VMEM((144, 1024), BF16), pltpu.VMEM((3, 384, 128), F32)],
         compiler_params=pltpu.CompilerParams(vmem_limit_bytes=32 << 20),
         name="gather_right",
-    )(core, recv, swap)
+    )(of, recv, swap)
 
 
 def contract_own_kernel(left_ref, right_ref, out_ref):
@@ -204,7 +210,9 @@
         y = jnp.dot(x_ref[...], swap_ref[:, n * 256 : n * 256 + 256], preferred_element_type=F32)
         for half in range(2):
             for s in range(18):
-                wide_ref[rows_of(s, 2 * n + half, 18), :] = y[s * 16 : s * 16 + 16, half * 128 : half * 128 + 128]
+                for zl in range(2):
+                    at = s * 16 + zl * 8
+                    wide_ref[rows_of(s, 2 * n + half, zl, 18), :] = y[at : at + 8, half * 128 : half * 128 + 128]
     out_ref[...] = wide_ref[...].astype(BF16)
 
 
@@ -258,15 +266,15 @@
     hold = lax.optimization_barrier
     sent, gate = project(pair, pair_mask, ln_gain.reshape(1, 128), ln_bias.reshape(1, 128), w_proj, w_gate)
     core = lax.axis_index("core").astype(jnp.int32).reshape(1)
-    sent, gate, core = hold((sent, gate, core))
+    sent, gate, core, other = hold((sent, gate, core, 1 - core))
     recv, gate, w_out, out_gain, out_bias = hold((exchange(sent), gate, w_out, out_gain, out_bias))
     place = np.arange(1024)
     swap = jnp.asarray(place[None, :] == (place // 16 % 8 * 128 + place // 128 * 16 + place % 16)[:, None], BF16)
     swap_cores = lambda v: lax.ppermute(v, "core", [(0, 1), (1, 0)])
     left = gather_left(recv, swap)
     left2 = swap_cores(left)
-    right_send, right = gather_right(core, recv, swap)
-    right2 = swap_cores(right_send)
+    right2 = swap_cores(gather_right(other, recv, swap))
+    right = gather_right(core, recv, swap)
     own = contract_own(left, right)
     sent = contract(own, left2, right2, swap)
     sent, gate, w_out, out_gain, out_bias = hold((sent, gate, w_out, out_gain, out_bias))

time: 86 us -> 84.9 us (0.987)
  blocking collectives: 75.9 us -> 74.5 us
    all_to_all x2, blocking collectives: 75.9 us -> 74.5 us  [exchange(): lax.all_to_all(tiles, GROUP, 0, 0, tiled=True).reshape(128 * rows, 128)]
  transfers between devices with their start and end apart: 2 -> 2, of which waited for: 1 -> 0; matrix products, arithmetic and copies ran while one was open for 0% -> 0% of each run, Pallas kernels for 2% -> 3%
where the time goes in v6:
time: 84.9 us; the launch traced here: 84.1 us
  blocking collectives  74.5 us (88%)
  Pallas kernels  8.84 us (10%)
    all_to_all x2, blocking collectives, exchange(): lax.all_to_all(tiles, GROUP, 0, 0, tiled=True).reshape(128 * rows, 128)  74.5 us
    pallas_call x1, Pallas kernels, project(): pl.pallas_call(project_kernel, out_shape=(pltpu.VMEM((4608, 128), BF16),...  2.84 us
  transfers between devices with their start and end apart: 2, of which 0 were waited for; matrix products, arithmetic and copies ran while one was open for 0% of the time, Pallas kernels for 3%

profile of v6, /device:TPU:32, one launch (start us, length us, event | category | flops | bytes accessed | tf_op | source)
XLA Modules:
  0.0 84.1 jit_solution(11876203124526616401)
XLA Ops:
  0.0 2.8 %project.1 = (bf16[4608,128]{1,0:T(8,128)(2,1)S(1)}, f32[48,48,128]{2,1,0:T(8,128)S(1)}) custom-call(f32[48,48,128]{2,1,0:T(8,128)} %pair_hbm.1, s32[48,48]{1,0:T(8,128)} %mask_hbm.1, f32[1,128]{1,0:T(1,128)} %bitcast.17, f32[1,128]{1,0:T(1,128)} %bitcast.18, bf16[128,512]{1,0:T(8,128)(2,1)} %w_hbm.1, bf16[128,128]{1,0:T(8,128)(2,1)} %w_gate_hbm.1), custom_call_target="tpu_custom_call" | custom-call | tf_op jit(solution)/shard_map/project/pallas_call | solution.py:104
  2.9 0.0 copy-start
  2.9 46.6 %all_to_all.10 = bf16[128,9,4,128]{3,2,1,0:T(4,128)(2,1)S(1)} all-to-all(bf16[128,9,4,128]{3,2,1,0:T(4,128)(2,1)S(1)} %bitcast.14), channel_id=1, replica_groups=mesh['xh'=2,'zh'=4,'zl'=2,'xl'=2,'y'=4,'core'=2] {'zl','y','zh','xh','xl'}, dimensions={0} | all-to-all | bytes 2359296 | tf_op jit(solution)/shard_map/all_to_all | solution.py:262
  49.5 0.0 copy-done
  49.5 0.9 %gather_left.1.left_ref = bf16[768,384]{1,0:T(8,128)(2,1)S(1)} custom-call(bf16[4608,128]{1,0:T(8,128)(2,1)S(1)} %bitcast.9, bf16[1024,1024]{1,0:T(8,128)(2,1)S(1)} %copy-done), custom_call_target="tpu_custom_call" | custom-call | tf_op jit(solution)/shard_map/gather_left/pallas_call | solution.py:162
  50.4 0.1 collective-permute-start
  50.5 0.7 gather_right.3
  51.3 0.6 collective-permute-start.1
  51.9 0.7 gather_right.2.right_ref
  52.6 0.7 contract_own.1.own_ref
  53.3 0.0 collective-permute-done.1.right_ref
  53.3 0.0 collective-permute-done.left_ref
  53.3 1.4 %contract.1 = bf16[2304,128]{1,0:T(8,128)(2,1)S(1)} custom-call(f32[768,384]{1,0:T(8,128)S(1)} %contract_own.1.own_ref, bf16[768,384]{1,0:T(8,128)(2,1)S(1)} %collective-permute-done.left_ref, bf16[384,384]{1,0:T(8,128)(2,1)S(1)} %collective-permute-done.1.right_ref, bf16[1024,1024]{1,0:T(8,128)(2,1)S(1)} %copy-done), custom_call_target="tpu_custom_call" | custom-call | tf_op jit(solution)/shard_map/contract/pallas_call | solution.py:220
  54.7 0.0 copy-start.1
  54.7 0.0 copy-start.2
  54.7 0.0 copy-start.3
  54.7 27.9 %all_to_all.11 = bf16[128,9,2,128]{3,2,1,0:T(2,128)(2,1)S(1)} all-to-all(bf16[128,9,2,128]{3,2,1,0:T(2,128)(2,1)S(1)} %bitcast.12), channel_id=1, replica_groups=mesh['xh'=2,'zh'=4,'zl'=2,'xl'=2,'y'=4,'core'=2] {'zl','y','zh','xh','xl'}, dimensions={0} | all-to-all | bytes 1179648 | tf_op jit(solution)/shard_map/all_to_all | solution.py:262
  82.6 0.0 copy-done.1
  82.6 0.0 copy-done.2
  82.6 0.0 copy-done.3
  82.6 1.6 %finish.1 = f32[48,48,128]{2,1,0:T(8,128)} custom-call(bf16[2304,128]{1,0:T(8,128)(2,1)S(1)} %bitcast.13, f32[48,48,128]{2,1,0:T(8,128)S(1)} %get-tuple-element.43.gate_ref, f32[1,128]{1,0:T(1,128)S(1)} %bitcast.15, f32[1,128]{1,0:T(1,128)S(1)} %bitcast.16, bf16[128,128]{1,0:T(8,128)(2,1)S(1)} %copy-done.1), custom_call_target="tpu_custom_call" | custom-call | tf_op jit(solution)/shard_map/finish/pallas_call | solution.py:248
Async XLA Ops:
  2.9 46.7 %copy-start = (bf16[1024,1024]{1,0:T(8,128)(2,1)S(1)}, bf16[1024,1024]{1,0:T(8,128)(2,1)}, u32[]{:S(2)}) copy-start(bf16[1024,1024]{1,0:T(8,128)(2,1)} %constant.8.clone.swap_ref) | copy-start | bytes 6291460
  50.4 2.9 %collective-permute-start = (bf16[768,384]{1,0:T(8,128)(2,1)S(1)}, bf16[768,384]{1,0:T(8,128)(2,1)S(1)}, u32[]{:S(2)}, u32[]{:S(2)}) collective-permute-start(bf16[768,384]{1,0:T(8,128)(2,1)S(1)} %gather_left.1.left_ref), channel_id=1, source_target_pairs={{0,1},{1,0},{2,3},{3,2},{4,5},{5,4},{6,7},{7,6},{8,9},{9,8},{10,11... | collective-permute-start | bytes 1769480 | tf_op jit(solution)/shard_map/ppermute | solution.py:273
  51.3 2.0 %collective-permute-start.1 = (bf16[384,384]{1,0:T(8,128)(2,1)S(1)}, bf16[384,384]{1,0:T(8,128)(2,1)S(1)}, u32[]{:S(2)}, u32[]{:S(2)}) collective-permute-start(bf16[384,384]{1,0:T(8,128)(2,1)S(1)} %gather_right.3), channel_id=1, source_target_pairs={{0,1},{1,0},{2,3},{3,2},{4,5},{5,4},{6,7},{7,6},{8,9},{9,8},{10,11... | collective-permute-start | bytes 884744 | tf_op jit(solution)/shard_map/ppermute | solution.py:273
  54.7 27.9 %copy-start.1 = (bf16[128,128]{1,0:T(8,128)(2,1)S(1)}, bf16[128,128]{1,0:T(8,128)(2,1)}, u32[]{:S(2)}) copy-start(bf16[128,128]{1,0:T(8,128)(2,1)} %w_ref) | copy-start | bytes 98308
  54.7 27.9 %copy-start.2 = (f32[128]{0:T(128)S(1)}, f32[128]{0:T(128)}, u32[]{:S(2)}) copy-start(f32[128]{0:T(128)} %param.16) | copy-start | bytes 1540
  54.7 27.9 %copy-start.3 = (f32[128]{0:T(128)S(1)}, f32[128]{0:T(128)}, u32[]{:S(2)}) copy-start(f32[128]{0:T(128)} %param.17) | copy-start | bytes 1540

commit v7 on v6

--- a/solution.py
+++ b/solution.py
@@ -11,13 +11,14 @@
 EPS = 1e-05
 ROW = ("xh", "zh", "zl")
 COL = ("xl", "y", "core")
-GROUP = ('zl', 'y', 'zh', 'xh', 'xl')
+GROUP = ("zl", "y", "zh", "xh", "xl")
 SIZES = dict(zh=4, zl=2, xl=2, y=4, xh=2)
 STEP = {axis: math.prod(SIZES[later] for later in GROUP[n + 1 :]) for n, axis in enumerate(GROUP)}
 XH_FIRST = GROUP.index("xh") < GROUP.index("zh")
 B_STEP = STEP["zh" if XH_FIRST else "xh"]
 PAIR = [STEP["y"] * (c % 4 if XH_FIRST else c // 2) + STEP["xl"] * (c // 4 if XH_FIRST else c % 2) for c in range(8)]
 F32, BF16 = jnp.float32, jnp.bfloat16
+SPARE = 128
 NT = (((1,), (1,)), ((), ()))
 TN = (((0,), (0,)), ((), ()))
 
@@ -97,7 +98,7 @@
                 wide_ref[pl.ds(at, 128, stride=36), :] = out[:, kk_hi * 128 : kk_hi * 128 + 128]
         gate = sigmoid(lax.dot_general(normed, w_gate_ref[...], TN, preferred_element_type=F32))
         gate_ref[part * 8 : part * 8 + 8] = gate.reshape(3, 8, 16, 128).transpose(1, 0, 2, 3).reshape(8, 48, 128)
-    out_ref[...] = wide_ref[...].astype(BF16)
+    out_ref[...] = wide_ref[:4608, :].astype(BF16)
 
 
 def project(pair, mask, gain, bias, w_proj, w_gate):
@@ -115,7 +116,7 @@
             pltpu.VMEM((128, 128), BF16),
             pltpu.VMEM((512, 128), BF16),
             pltpu.VMEM((6, 128, 384), BF16),
-            pltpu.VMEM((4608, 128), F32),
+            pltpu.VMEM((4608 + SPARE, 128), F32),
             pltpu.SemaphoreType.DMA((11,)),
         ],
         compiler_params=pltpu.CompilerParams(vmem_limit_bytes=32 << 20),
@@ -124,7 +125,7 @@
 
 
 def gather_left_kernel(recv_ref, swap_ref, out_ref, wide_ref, x_ref):
-    wide_ref[...] = recv_ref[...].astype(F32)
+    wide_ref[:4608, :] = recv_ref[...].astype(F32)
     for s in range(18):
         for c in range(8):
             rows = [wide_ref[rows_of(s, c, zl, 36), :] for zl in range(2)]
@@ -139,10 +140,10 @@
 
 
 def gather_right_kernel(of_ref, recv_ref, swap_ref, out_ref, wide_ref, x_ref, rows_ref):
-    wide_ref[...] = recv_ref[...].astype(F32)
+    wide_ref[:2304, :] = recv_ref[pl.ds(pl.multiple_of(of_ref[0] * 2304, 2304), 2304), :].astype(F32)
     for s in range(0, 18, 2):
         for c in range(8):
-            rows = [wide_ref[rows_of(18 + s + k, c, of_ref[0], 36), :] for k in range(2)]
+            rows = [wide_ref[rows_of(18 + s + k, c, 0, 36), :] for k in range(2)]
             x_ref[s * 8 : s * 8 + 16, c * 128 : c * 128 + 128] = jnp.concatenate(rows).astype(BF16)
     for n in range(4):
         y = jnp.dot(x_ref[...], swap_ref[:, n * 256 : n * 256 + 256], preferred_element_type=F32)
@@ -162,7 +163,7 @@
     return pl.pallas_call(
         gather_left_kernel,
         out_shape=jax.ShapeDtypeStruct((768, 384), BF16),
-        scratch_shapes=[pltpu.VMEM((4608, 128), F32), pltpu.VMEM((288, 1024), BF16)],
+        scratch_shapes=[pltpu.VMEM((4608 + SPARE, 128), F32), pltpu.VMEM((288, 1024), BF16)],
         compiler_params=pltpu.CompilerParams(vmem_limit_bytes=32 << 20),
         name="gather_left",
     )(recv, swap)
@@ -175,7 +176,11 @@
         out_shape=jax.ShapeDtypeStruct((384, 384), BF16),
         in_specs=[pl.BlockSpec(memory_space=pltpu.SMEM), vmem, vmem],
         out_specs=vmem,
-        scratch_shapes=[pltpu.VMEM((4608, 128), F32), pltpu.VMEM((144, 1024), BF16), pltpu.VMEM((3, 384, 128), F32)],
+        scratch_shapes=[
+            pltpu.VMEM((2304 + SPARE, 128), F32),
+            pltpu.VMEM((144, 1024), BF16),
+            pltpu.VMEM((3, 384 + SPARE, 128), F32),
+        ],
         compiler_params=pltpu.CompilerParams(vmem_limit_bytes=32 << 20),
         name="gather_right",
     )(of, recv, swap)
@@ -213,21 +218,21 @@
                 for zl in range(2):
                     at = s * 16 + zl * 8
                     wide_ref[rows_of(s, 2 * n + half, zl, 18), :] = y[at : at + 8, half * 128 : half * 128 + 128]
-    out_ref[...] = wide_ref[...].astype(BF16)
+    out_ref[...] = wide_ref[:2304, :].astype(BF16)
 
 
 def contract(own, left, right, swap):
     return pl.pallas_call(
         contract_kernel,
         out_shape=jax.ShapeDtypeStruct((2304, 128), BF16),
-        scratch_shapes=[pltpu.VMEM((288, 1024), BF16), pltpu.VMEM((2304, 128), F32)],
+        scratch_shapes=[pltpu.VMEM((288, 1024), BF16), pltpu.VMEM((2304 + SPARE, 128), F32)],
         compiler_params=pltpu.CompilerParams(vmem_limit_bytes=32 << 20),
         name="contract",
     )(own, left, right, swap)
 
 
 def finish_kernel(mixed_ref, gate_ref, gain_ref, bias_ref, w_ref, out_hbm, wide_ref, out_ref, sems):
-    wide_ref[...] = mixed_ref[...].astype(F32)
+    wide_ref[:2304, :] = mixed_ref[...].astype(F32)
     gain, bias = column(gain_ref[...]), column(bias_ref[...])
     copies = []
     for part in range(6):
@@ -250,7 +255,11 @@
         out_shape=jax.ShapeDtypeStruct((48, 48, 128), F32),
         in_specs=[pl.BlockSpec(memory_space=pltpu.VMEM)] * 5,
         out_specs=pl.BlockSpec(memory_space=pltpu.HBM),
-        scratch_shapes=[pltpu.VMEM((2304, 128), F32), pltpu.VMEM((48, 48, 128), F32), pltpu.SemaphoreType.DMA((6,))],
+        scratch_shapes=[
+            pltpu.VMEM((2304 + SPARE, 128), F32),
+            pltpu.VMEM((48, 48, 128), F32),
+            pltpu.SemaphoreType.DMA((6,)),
+        ],
         compiler_params=pltpu.CompilerParams(vmem_limit_bytes=32 << 20),
         name="finish",
     )(mixed, gate, gain, bias, w_out)

time: 84.9 us -> 84.9 us (level)
  transfers between devices with their start and end apart: 2 -> 2, of which waited for: 0 -> 0; matrix products, arithmetic and copies ran while one was open for 0% -> 0% of each run, Pallas kernels for 3% -> 2%
where the time goes in v7:
time: 84.9 us; the launch traced here: 84 us
  blocking collectives  74.6 us (88%)
  Pallas kernels  8.59 us (10%)
    all_to_all x2, blocking collectives, exchange(): lax.all_to_all(tiles, GROUP, 0, 0, tiled=True).reshape(128 * rows, 128)  74.6 us
    pallas_call x1, Pallas kernels, project(): pl.pallas_call(project_kernel, out_shape=(pltpu.VMEM((4608, 128), BF16),...  2.84 us
  transfers between devices with their start and end apart: 2, of which 0 were waited for; matrix products, arithmetic and copies ran while one was open for 0% of the time, Pallas kernels for 2%

profile of v7, /device:TPU:32, one launch (start us, length us, event | category | flops | bytes accessed | tf_op | source)
XLA Modules:
  0.0 84.0 jit_solution(8698176444225562252)
XLA Ops:
  0.0 2.8 %project.1 = (bf16[4608,128]{1,0:T(8,128)(2,1)S(1)}, f32[48,48,128]{2,1,0:T(8,128)S(1)}) custom-call(f32[48,48,128]{2,1,0:T(8,128)} %pair_hbm.1, s32[48,48]{1,0:T(8,128)} %mask_hbm.1, f32[1,128]{1,0:T(1,128)} %bitcast.17, f32[1,128]{1,0:T(1,128)} %bitcast.18, bf16[128,512]{1,0:T(8,128)(2,1)} %w_hbm.1, bf16[128,128]{1,0:T(8,128)(2,1)} %w_gate_hbm.1), custom_call_target="tpu_custom_call" | custom-call | tf_op jit(solution)/shard_map/project/pallas_call | solution.py:105
  2.9 0.0 copy-start
  2.9 46.6 %all_to_all.10 = bf16[128,9,4,128]{3,2,1,0:T(4,128)(2,1)S(1)} all-to-all(bf16[128,9,4,128]{3,2,1,0:T(4,128)(2,1)S(1)} %bitcast.14), channel_id=1, replica_groups=mesh['xh'=2,'zh'=4,'zl'=2,'xl'=2,'y'=4,'core'=2] {'zl','y','zh','xh','xl'}, dimensions={0} | all-to-all | bytes 2359296 | tf_op jit(solution)/shard_map/all_to_all | solution.py:271
  49.5 0.0 copy-done
  49.5 0.9 %gather_left.1.left_ref = bf16[768,384]{1,0:T(8,128)(2,1)S(1)} custom-call(bf16[4608,128]{1,0:T(8,128)(2,1)S(1)} %bitcast.9, bf16[1024,1024]{1,0:T(8,128)(2,1)S(1)} %copy-done), custom_call_target="tpu_custom_call" | custom-call | tf_op jit(solution)/shard_map/gather_left/pallas_call | solution.py:163
  50.4 0.1 collective-permute-start
  50.5 0.6 gather_right.3
  51.1 0.6 collective-permute-start.1
  51.7 0.6 gather_right.2.right_ref
  52.3 0.7 contract_own.1.own_ref
  53.0 0.0 collective-permute-done.1.right_ref
  53.0 0.0 collective-permute-done.left_ref
  53.0 1.4 %contract.1 = bf16[2304,128]{1,0:T(8,128)(2,1)S(1)} custom-call(f32[768,384]{1,0:T(8,128)S(1)} %contract_own.1.own_ref, bf16[768,384]{1,0:T(8,128)(2,1)S(1)} %collective-permute-done.left_ref, bf16[384,384]{1,0:T(8,128)(2,1)S(1)} %collective-permute-done.1.right_ref, bf16[1024,1024]{1,0:T(8,128)(2,1)S(1)} %copy-done), custom_call_target="tpu_custom_call" | custom-call | tf_op jit(solution)/shard_map/contract/pallas_call | solution.py:225
  54.4 0.0 copy-start.1
  54.4 0.0 copy-start.2
  54.4 0.0 copy-start.3
  54.5 28.0 %all_to_all.11 = bf16[128,9,2,128]{3,2,1,0:T(2,128)(2,1)S(1)} all-to-all(bf16[128,9,2,128]{3,2,1,0:T(2,128)(2,1)S(1)} %bitcast.12), channel_id=1, replica_groups=mesh['xh'=2,'zh'=4,'zl'=2,'xl'=2,'y'=4,'core'=2] {'zl','y','zh','xh','xl'}, dimensions={0} | all-to-all | bytes 1179648 | tf_op jit(solution)/shard_map/all_to_all | solution.py:271
  82.4 0.0 copy-done.1
  82.4 0.0 copy-done.2
  82.4 0.0 copy-done.3
  82.4 1.6 %finish.1 = f32[48,48,128]{2,1,0:T(8,128)} custom-call(bf16[2304,128]{1,0:T(8,128)(2,1)S(1)} %bitcast.13, f32[48,48,128]{2,1,0:T(8,128)S(1)} %get-tuple-element.43.gate_ref, f32[1,128]{1,0:T(1,128)S(1)} %bitcast.15, f32[1,128]{1,0:T(1,128)S(1)} %bitcast.16, bf16[128,128]{1,0:T(8,128)(2,1)S(1)} %copy-done.1), custom_call_target="tpu_custom_call" | custom-call | tf_op jit(solution)/shard_map/finish/pallas_call | solution.py:253
Async XLA Ops:
  2.9 46.7 %copy-start = (bf16[1024,1024]{1,0:T(8,128)(2,1)S(1)}, bf16[1024,1024]{1,0:T(8,128)(2,1)}, u32[]{:S(2)}) copy-start(bf16[1024,1024]{1,0:T(8,128)(2,1)} %constant.8.clone.swap_ref) | copy-start | bytes 6291460
  50.4 2.6 %collective-permute-start = (bf16[768,384]{1,0:T(8,128)(2,1)S(1)}, bf16[768,384]{1,0:T(8,128)(2,1)S(1)}, u32[]{:S(2)}, u32[]{:S(2)}) collective-permute-start(bf16[768,384]{1,0:T(8,128)(2,1)S(1)} %gather_left.1.left_ref), channel_id=1, source_target_pairs={{0,1},{1,0},{2,3},{3,2},{4,5},{5,4},{6,7},{7,6},{8,9},{9,8},{10,11... | collective-permute-start | bytes 1769480 | tf_op jit(solution)/shard_map/ppermute | solution.py:282
  51.1 1.9 %collective-permute-start.1 = (bf16[384,384]{1,0:T(8,128)(2,1)S(1)}, bf16[384,384]{1,0:T(8,128)(2,1)S(1)}, u32[]{:S(2)}, u32[]{:S(2)}) collective-permute-start(bf16[384,384]{1,0:T(8,128)(2,1)S(1)} %gather_right.3), channel_id=1, source_target_pairs={{0,1},{1,0},{2,3},{3,2},{4,5},{5,4},{6,7},{7,6},{8,9},{9,8},{10,11... | collective-permute-start | bytes 884744 | tf_op jit(solution)/shard_map/ppermute | solution.py:282
  54.4 28.0 %copy-start.1 = (bf16[128,128]{1,0:T(8,128)(2,1)S(1)}, bf16[128,128]{1,0:T(8,128)(2,1)}, u32[]{:S(2)}) copy-start(bf16[128,128]{1,0:T(8,128)(2,1)} %w_ref) | copy-start | bytes 98308
  54.4 28.0 %copy-start.2 = (f32[128]{0:T(128)S(1)}, f32[128]{0:T(128)}, u32[]{:S(2)}) copy-start(f32[128]{0:T(128)} %param.16) | copy-start | bytes 1540
  54.4 28.0 %copy-start.3 = (f32[128]{0:T(128)S(1)}, f32[128]{0:T(128)}, u32[]{:S(2)}) copy-start(f32[128]{0:T(128)} %param.17) | copy-start | bytes 1540

commit v8 on v7

--- a/solution.py
+++ b/solution.py
@@ -66,17 +66,19 @@
         pltpu.make_async_copy(pair_hbm.at[pl.ds(part * 8, 8)], pair_ref.at[pl.ds(part * 8, 8)], sems.at[part])
         for part in range(6)
     ]
-    for copy in chunks[:2] + small + chunks[2:]:
+    for copy in small + chunks:
         copy.start()
     lane = lax.broadcasted_iota(jnp.int32, (48, 384), 1)
     row = lax.broadcasted_iota(jnp.int32, (48, 384), 0)
     spread = (lane // 128 * 16 + lane % 16 == row).astype(F32).astype(BF16)
     own = lax.broadcasted_iota(jnp.int32, (8, 384), 1) // 16 % 8 == lax.broadcasted_iota(jnp.int32, (8, 384), 0)
-    for copy in small + chunks[:2]:
+    for copy in small:
         copy.wait()
     wt_ref[...] = w_ref[...].astype(F32).T.astype(BF16)
     keeps = jnp.dot(mask_ref[...].astype(F32).astype(BF16), spread, preferred_element_type=F32)
     gain, bias = column(gain_ref[...]), column(bias_ref[...])
+    for copy in chunks[:2]:
+        copy.wait()
 
     def norm(part):
         x = pair_ref[part * 8 : part * 8 + 8].reshape(8, 3, 16, 128).transpose(1, 0, 2, 3).reshape(384, 128)
@@ -280,9 +282,8 @@
     place = np.arange(1024)
     swap = jnp.asarray(place[None, :] == (place // 16 % 8 * 128 + place // 128 * 16 + place % 16)[:, None], BF16)
     swap_cores = lambda v: lax.ppermute(v, "core", [(0, 1), (1, 0)])
-    left = gather_left(recv, swap)
-    left2 = swap_cores(left)
-    right2 = swap_cores(gather_right(other, recv, swap))
+    left, right2 = hold((gather_left(recv, swap), gather_right(other, recv, swap)))
+    left2, right2 = swap_cores(left), swap_cores(right2)
     right = gather_right(core, recv, swap)
     own = contract_own(left, right)
     sent = contract(own, left2, right2, swap)

time: 84.9 us -> 85.2 us (level)
  transfers between devices with their start and end apart: 2 -> 2, of which waited for: 0 -> 1; matrix products, arithmetic and copies ran while one was open for 0% -> 0% of each run, Pallas kernels for 2% -> 2%
where the time goes in v8:
time: 85.2 us; the launch traced here: 84.4 us
  blocking collectives  74.5 us (87%)
  Pallas kernels  8.57 us (10%)
    all_to_all x2, blocking collectives, exchange(): lax.all_to_all(tiles, GROUP, 0, 0, tiled=True).reshape(128 * rows, 128)  74.5 us
    pallas_call x1, Pallas kernels, project(): pl.pallas_call(project_kernel, out_shape=(pltpu.VMEM((4608, 128), BF16),...  2.82 us
  transfers between devices with their start and end apart: 2, of which 1 were waited for; matrix products, arithmetic and copies ran while one was open for 0% of the time, Pallas kernels for 2%

profile of v8, /device:TPU:32, one launch (start us, length us, event | category | flops | bytes accessed | tf_op | source)
XLA Modules:
  0.0 84.4 jit_solution(7311870147902636139)
XLA Ops:
  0.0 2.8 %project.1 = (bf16[4608,128]{1,0:T(8,128)(2,1)S(1)}, f32[48,48,128]{2,1,0:T(8,128)S(1)}) custom-call(f32[48,48,128]{2,1,0:T(8,128)} %pair_hbm.1, s32[48,48]{1,0:T(8,128)} %mask_hbm.1, f32[1,128]{1,0:T(1,128)} %bitcast.17, f32[1,128]{1,0:T(1,128)} %bitcast.18, bf16[128,512]{1,0:T(8,128)(2,1)} %w_hbm.1, bf16[128,128]{1,0:T(8,128)(2,1)} %w_gate_hbm.1), custom_call_target="tpu_custom_call" | custom-call | tf_op jit(solution)/shard_map/project/pallas_call | solution.py:107
  2.8 0.0 copy-start
  2.8 46.6 %all_to_all.10 = bf16[128,9,4,128]{3,2,1,0:T(4,128)(2,1)S(1)} all-to-all(bf16[128,9,4,128]{3,2,1,0:T(4,128)(2,1)S(1)} %bitcast.14), channel_id=1, replica_groups=mesh['xh'=2,'zh'=4,'zl'=2,'xl'=2,'y'=4,'core'=2] {'zl','y','zh','xh','xl'}, dimensions={0} | all-to-all | bytes 2359296 | tf_op jit(solution)/shard_map/all_to_all | solution.py:273
  49.5 0.0 copy-done
  49.5 0.9 %gather_left.1.left_ref = bf16[768,384]{1,0:T(8,128)(2,1)S(1)} custom-call(bf16[4608,128]{1,0:T(8,128)(2,1)S(1)} %bitcast.9, bf16[1024,1024]{1,0:T(8,128)(2,1)S(1)} %copy-done), custom_call_target="tpu_custom_call" | custom-call | tf_op jit(solution)/shard_map/gather_left/pallas_call | solution.py:165
  50.4 0.6 gather_right.2
  51.0 0.1 collective-permute-start
  51.1 0.5 collective-permute-start.1
  51.6 0.6 gather_right.3.right_ref
  52.2 0.7 contract_own.1.own_ref
  52.9 0.6 collective-permute-done.1.right_ref
  53.5 0.0 collective-permute-done.left_ref
  53.5 1.4 %contract.1 = bf16[2304,128]{1,0:T(8,128)(2,1)S(1)} custom-call(f32[768,384]{1,0:T(8,128)S(1)} %contract_own.1.own_ref, bf16[768,384]{1,0:T(8,128)(2,1)S(1)} %collective-permute-done.left_ref, bf16[384,384]{1,0:T(8,128)(2,1)S(1)} %collective-permute-done.1.right_ref, bf16[1024,1024]{1,0:T(8,128)(2,1)S(1)} %copy-done), custom_call_target="tpu_custom_call" | custom-call | tf_op jit(solution)/shard_map/contract/pallas_call | solution.py:227
  54.9 0.0 copy-start.1
  54.9 0.0 copy-start.2
  54.9 0.0 copy-start.3
  54.9 27.8 %all_to_all.11 = bf16[128,9,2,128]{3,2,1,0:T(2,128)(2,1)S(1)} all-to-all(bf16[128,9,2,128]{3,2,1,0:T(2,128)(2,1)S(1)} %bitcast.12), channel_id=1, replica_groups=mesh['xh'=2,'zh'=4,'zl'=2,'xl'=2,'y'=4,'core'=2] {'zl','y','zh','xh','xl'}, dimensions={0} | all-to-all | bytes 1179648 | tf_op jit(solution)/shard_map/all_to_all | solution.py:273
  82.8 0.0 copy-done.1
  82.8 0.0 copy-done.2
  82.8 0.0 copy-done.3
  82.8 1.6 %finish.1 = f32[48,48,128]{2,1,0:T(8,128)} custom-call(bf16[2304,128]{1,0:T(8,128)(2,1)S(1)} %bitcast.13, f32[48,48,128]{2,1,0:T(8,128)S(1)} %get-tuple-element.47.gate_ref, f32[1,128]{1,0:T(1,128)S(1)} %bitcast.15, f32[1,128]{1,0:T(1,128)S(1)} %bitcast.16, bf16[128,128]{1,0:T(8,128)(2,1)S(1)} %copy-done.1), custom_call_target="tpu_custom_call" | custom-call | tf_op jit(solution)/shard_map/finish/pallas_call | solution.py:255
Async XLA Ops:
  2.8 46.7 %copy-start = (bf16[1024,1024]{1,0:T(8,128)(2,1)S(1)}, bf16[1024,1024]{1,0:T(8,128)(2,1)}, u32[]{:S(2)}) copy-start(bf16[1024,1024]{1,0:T(8,128)(2,1)} %constant.8.clone.swap_ref) | copy-start | bytes 6291460
  51.0 2.5 %collective-permute-start = (bf16[768,384]{1,0:T(8,128)(2,1)S(1)}, bf16[768,384]{1,0:T(8,128)(2,1)S(1)}, u32[]{:S(2)}, u32[]{:S(2)}) collective-permute-start(bf16[768,384]{1,0:T(8,128)(2,1)S(1)} %gather_left.1.left_ref), channel_id=1, source_target_pairs={{0,1},{1,0},{2,3},{3,2},{4,5},{5,4},{6,7},{7,6},{8,9},{9,8},{10,11... | collective-permute-start | bytes 1769480 | tf_op jit(solution)/shard_map/ppermute | solution.py:284
  51.1 2.4 %collective-permute-start.1 = (bf16[384,384]{1,0:T(8,128)(2,1)S(1)}, bf16[384,384]{1,0:T(8,128)(2,1)S(1)}, u32[]{:S(2)}, u32[]{:S(2)}) collective-permute-start(bf16[384,384]{1,0:T(8,128)(2,1)S(1)} %gather_right.2), channel_id=1, source_target_pairs={{0,1},{1,0},{2,3},{3,2},{4,5},{5,4},{6,7},{7,6},{8,9},{9,8},{10,11... | collective-permute-start | bytes 884744 | tf_op jit(solution)/shard_map/ppermute | solution.py:284
  54.9 27.9 %copy-start.1 = (bf16[128,128]{1,0:T(8,128)(2,1)S(1)}, bf16[128,128]{1,0:T(8,128)(2,1)}, u32[]{:S(2)}) copy-start(bf16[128,128]{1,0:T(8,128)(2,1)} %w_ref) | copy-start | bytes 98308
  54.9 27.9 %copy-start.2 = (f32[128]{0:T(128)S(1)}, f32[128]{0:T(128)}, u32[]{:S(2)}) copy-start(f32[128]{0:T(128)} %param.16) | copy-start | bytes 1540
  54.9 27.9 %copy-start.3 = (f32[128]{0:T(128)S(1)}, f32[128]{0:T(128)}, u32[]{:S(2)}) copy-start(f32[128]{0:T(128)} %param.17) | copy-start | bytes 1540

commit v9 on v8

--- a/solution.py
+++ b/solution.py
@@ -282,8 +282,9 @@
     place = np.arange(1024)
     swap = jnp.asarray(place[None, :] == (place // 16 % 8 * 128 + place // 128 * 16 + place % 16)[:, None], BF16)
     swap_cores = lambda v: lax.ppermute(v, "core", [(0, 1), (1, 0)])
-    left, right2 = hold((gather_left(recv, swap), gather_right(other, recv, swap)))
-    left2, right2 = swap_cores(left), swap_cores(right2)
+    left = gather_left(recv, swap)
+    left2 = swap_cores(left)
+    right2 = swap_cores(gather_right(other, recv, swap))
     right = gather_right(core, recv, swap)
     own = contract_own(left, right)
     sent = contract(own, left2, right2, swap)

time: 85.2 us -> 84.9 us (level)
  transfers between devices with their start and end apart: 2 -> 2, of which waited for: 1 -> 0; matrix products, arithmetic and copies ran while one was open for 0% -> 0% of each run, Pallas kernels for 2% -> 2%
where the time goes in v9:
time: 84.9 us; the launch traced here: 84 us
  blocking collectives  74.6 us (88%)
  Pallas kernels  8.57 us (10%)
    all_to_all x2, blocking collectives, exchange(): lax.all_to_all(tiles, GROUP, 0, 0, tiled=True).reshape(128 * rows, 128)  74.6 us
    pallas_call x1, Pallas kernels, project(): pl.pallas_call(project_kernel, out_shape=(pltpu.VMEM((4608, 128), BF16),...  2.82 us
  transfers between devices with their start and end apart: 2, of which 0 were waited for; matrix products, arithmetic and copies ran while one was open for 0% of the time, Pallas kernels for 2%

profile of v9, /device:TPU:32, one launch (start us, length us, event | category | flops | bytes accessed | tf_op | source)
XLA Modules:
  0.0 84.0 jit_solution(11932080713225100159)
XLA Ops:
  0.0 2.8 %project.1 = (bf16[4608,128]{1,0:T(8,128)(2,1)S(1)}, f32[48,48,128]{2,1,0:T(8,128)S(1)}) custom-call(f32[48,48,128]{2,1,0:T(8,128)} %pair_hbm.1, s32[48,48]{1,0:T(8,128)} %mask_hbm.1, f32[1,128]{1,0:T(1,128)} %bitcast.17, f32[1,128]{1,0:T(1,128)} %bitcast.18, bf16[128,512]{1,0:T(8,128)(2,1)} %w_hbm.1, bf16[128,128]{1,0:T(8,128)(2,1)} %w_gate_hbm.1), custom_call_target="tpu_custom_call" | custom-call | tf_op jit(solution)/shard_map/project/pallas_call | solution.py:107
  2.8 0.0 copy-start
  2.8 46.6 %all_to_all.10 = bf16[128,9,4,128]{3,2,1,0:T(4,128)(2,1)S(1)} all-to-all(bf16[128,9,4,128]{3,2,1,0:T(4,128)(2,1)S(1)} %bitcast.14), channel_id=1, replica_groups=mesh['xh'=2,'zh'=4,'zl'=2,'xl'=2,'y'=4,'core'=2] {'zl','y','zh','xh','xl'}, dimensions={0} | all-to-all | bytes 2359296 | tf_op jit(solution)/shard_map/all_to_all | solution.py:273
  49.5 0.0 copy-done
  49.5 0.9 %gather_left.1.left_ref = bf16[768,384]{1,0:T(8,128)(2,1)S(1)} custom-call(bf16[4608,128]{1,0:T(8,128)(2,1)S(1)} %bitcast.9, bf16[1024,1024]{1,0:T(8,128)(2,1)S(1)} %copy-done), custom_call_target="tpu_custom_call" | custom-call | tf_op jit(solution)/shard_map/gather_left/pallas_call | solution.py:165
  50.4 0.1 collective-permute-start
  50.5 0.6 gather_right.3
  51.1 0.6 collective-permute-start.1
  51.7 0.6 gather_right.2.right_ref
  52.3 0.7 contract_own.1.own_ref
  53.0 0.0 collective-permute-done.1.right_ref
  53.0 0.0 collective-permute-done.left_ref
  53.0 1.4 %contract.1 = bf16[2304,128]{1,0:T(8,128)(2,1)S(1)} custom-call(f32[768,384]{1,0:T(8,128)S(1)} %contract_own.1.own_ref, bf16[768,384]{1,0:T(8,128)(2,1)S(1)} %collective-permute-done.left_ref, bf16[384,384]{1,0:T(8,128)(2,1)S(1)} %collective-permute-done.1.right_ref, bf16[1024,1024]{1,0:T(8,128)(2,1)S(1)} %copy-done), custom_call_target="tpu_custom_call" | custom-call | tf_op jit(solution)/shard_map/contract/pallas_call | solution.py:227
  54.4 0.0 copy-start.1
  54.4 0.0 copy-start.2
  54.4 0.0 copy-start.3
  54.4 28.0 %all_to_all.11 = bf16[128,9,2,128]{3,2,1,0:T(2,128)(2,1)S(1)} all-to-all(bf16[128,9,2,128]{3,2,1,0:T(2,128)(2,1)S(1)} %bitcast.12), channel_id=1, replica_groups=mesh['xh'=2,'zh'=4,'zl'=2,'xl'=2,'y'=4,'core'=2] {'zl','y','zh','xh','xl'}, dimensions={0} | all-to-all | bytes 1179648 | tf_op jit(solution)/shard_map/all_to_all | solution.py:273
  82.4 0.0 copy-done.1
  82.4 0.0 copy-done.2
  82.4 0.0 copy-done.3
  82.4 1.6 %finish.1 = f32[48,48,128]{2,1,0:T(8,128)} custom-call(bf16[2304,128]{1,0:T(8,128)(2,1)S(1)} %bitcast.13, f32[48,48,128]{2,1,0:T(8,128)S(1)} %get-tuple-element.43.gate_ref, f32[1,128]{1,0:T(1,128)S(1)} %bitcast.15, f32[1,128]{1,0:T(1,128)S(1)} %bitcast.16, bf16[128,128]{1,0:T(8,128)(2,1)S(1)} %copy-done.1), custom_call_target="tpu_custom_call" | custom-call | tf_op jit(solution)/shard_map/finish/pallas_call | solution.py:255
Async XLA Ops:
  2.8 46.7 %copy-start = (bf16[1024,1024]{1,0:T(8,128)(2,1)S(1)}, bf16[1024,1024]{1,0:T(8,128)(2,1)}, u32[]{:S(2)}) copy-start(bf16[1024,1024]{1,0:T(8,128)(2,1)} %constant.8.clone.swap_ref) | copy-start | bytes 6291460
  50.4 2.6 %collective-permute-start = (bf16[768,384]{1,0:T(8,128)(2,1)S(1)}, bf16[768,384]{1,0:T(8,128)(2,1)S(1)}, u32[]{:S(2)}, u32[]{:S(2)}) collective-permute-start(bf16[768,384]{1,0:T(8,128)(2,1)S(1)} %gather_left.1.left_ref), channel_id=1, source_target_pairs={{0,1},{1,0},{2,3},{3,2},{4,5},{5,4},{6,7},{7,6},{8,9},{9,8},{10,11... | collective-permute-start | bytes 1769480 | tf_op jit(solution)/shard_map/ppermute | solution.py:284
  51.1 1.9 %collective-permute-start.1 = (bf16[384,384]{1,0:T(8,128)(2,1)S(1)}, bf16[384,384]{1,0:T(8,128)(2,1)S(1)}, u32[]{:S(2)}, u32[]{:S(2)}) collective-permute-start(bf16[384,384]{1,0:T(8,128)(2,1)S(1)} %gather_right.3), channel_id=1, source_target_pairs={{0,1},{1,0},{2,3},{3,2},{4,5},{5,4},{6,7},{7,6},{8,9},{9,8},{10,11... | collective-permute-start | bytes 884744 | tf_op jit(solution)/shard_map/ppermute | solution.py:284
  54.4 28.0 %copy-start.1 = (bf16[128,128]{1,0:T(8,128)(2,1)S(1)}, bf16[128,128]{1,0:T(8,128)(2,1)}, u32[]{:S(2)}) copy-start(bf16[128,128]{1,0:T(8,128)(2,1)} %w_ref) | copy-start | bytes 98308
  54.4 28.0 %copy-start.2 = (f32[128]{0:T(128)S(1)}, f32[128]{0:T(128)}, u32[]{:S(2)}) copy-start(f32[128]{0:T(128)} %param.16) | copy-start | bytes 1540
  54.4 28.0 %copy-start.3 = (f32[128]{0:T(128)S(1)}, f32[128]{0:T(128)}, u32[]{:S(2)}) copy-start(f32[128]{0:T(128)} %param.17) | copy-start | bytes 1540
